TPU v7x, 512 devices: a whole 4x8x8 slice. The times are simulated.
512 devices in a mesh: dp: 8 (over x, core), context: 16 (over y_lo, z), tensor: 4 (over y_hi).
Axes of the slice: x: 4, y: 8 (y_hi: 4, y_lo: 2; y = y_hi * 2 + y_lo), z: 8, core: 2. Of those that a mesh axis runs over, the one named last changes fastest.
Arguments:
- staying_cache: bfloat16 [16, 32, 256, 576], P('context', 'dp'), parts along dimension 1, may hold values from -6 to 6
- leaving_cache: bfloat16 [16, 32, 256, 576], P('context', 'dp'), parts along dimension 1, may hold values from -6 to 6
- lengths: int32 [32], P('dp'), parts along dimension 0, may hold values from 4096 to 8190, as said below
- pairing: int32 [32, 16], P('dp'), parts along dimension 0, may hold values from 0 to 15, as said below
- new_entries: bfloat16 [32, 2, 576], P('dp'), parts along dimension 0, may hold values from -6 to 6
- queries: bfloat16 [32, 2, 64, 576], P('dp', None, 'tensor'), parts along dimension 0, may hold values from -40 to 40
- w_value: bfloat16 [64, 512, 128], P('tensor', 'context'), may hold values from -2.390625 to 2.390625
- w_out: bfloat16 [8192, 7168], P('tensor', 'context'), may hold values from -0.0625 to 0.0625
Outputs:
- new_cache: bfloat16 [16, 32, 512, 576], P('context', 'dp'), parts along dimension 1
- attn_out: bfloat16 [32, 2, 7168], P('dp', None, ('context', 'tensor')), parts along dimension 0
There are 8 independent parts, one for each index of `dp`. A program takes and returns all parts, laid end to end along the dimension named above; an argument that names none is the same for every part. Nothing has to cross between parts.
Inputs may be any that keep to these rules, and one draw needn't show every extreme that they name: pairing[b, j] = (j + m_b) mod 16 for one offset m_b of each request b, the same for every j. `lengths`: every draw has a request of length 8190.
All inputs are finite; a program needn't handle non-finite values.
Results may differ from a plain program's by a relative error of at most 0.015.
Values may be sent and summed in bfloat16 or wider, within the bound.
No kernel may reach another device: no remote copies, remote signals or barrier semaphores. Data moves between devices by JAX's collectives and lax.ppermute only.
A program may use at most 128 MiB of HBM per device.

v0:
```python
import jax
import jax.numpy as jnp
from jax import lax
from jax.sharding import PartitionSpec as P

LATENT = 512


softmax_scale = 0.07216878364870322
large_negative = -1e30


def passed_along(block, axis, distance):
    devices = range(lax.axis_size(axis))
    route = [((i - distance) % len(devices), i) for i in devices]
    return lax.ppermute(block, axis, route)


def combined_all(value, axis, join):
    pieces = jax.tree.map(lambda part: lax.all_gather(part, axis), value)
    head = jax.tree.map(lambda part: part[0], pieces)
    tail = jax.tree.map(lambda part: part[1:], pieces)
    running, _ = lax.scan(lambda running, section: (join(running, section), None), head, tail)
    return running


def body(staying_cache, leaving_cache, lengths, pairing, new_entries, queries, w_value, w_out):
    members = lax.axis_size("context")
    member_index = lax.axis_index("context")
    offsets = pairing[:, 0]
    source = (member_index - offsets) % members
    slice_len = staying_cache.shape[2]
    arrived = leaving_cache
    for section_bit in range(members.bit_length() - 1):
        shifted = passed_along(arrived, "context", 1 << section_bit)
        taken = offsets >> section_bit & 1 == 1
        arrived = jnp.where(taken[None, :, None, None], shifted, arrived)
    new_cache = jnp.concatenate([staying_cache, arrived], axis=2)
    request_count = lengths.shape[0]
    slot_index = jnp.arange(slice_len, dtype=jnp.int32)
    own_positions = jnp.broadcast_to(
        (member_index * slice_len + slot_index)[None, :], (request_count, slice_len)
    )
    moved_positions = (members + source)[:, None] * slice_len + slot_index[None, :]
    slot_positions = jnp.concatenate([own_positions, moved_positions], axis=1)
    step_count = new_entries.shape[1]
    for step_number in range(step_count):
        target = slot_positions == (lengths + step_number)[:, None]
        new_cache = jnp.where(
            target[None, :, :, None], new_entries[None, :, step_number, None, :], new_cache
        )
    key_rows = new_cache[0]
    scores = (
        jnp.einsum("bthw,bjw->bthj", queries, key_rows, preferred_element_type=jnp.float32)
        * softmax_scale
    )
    step_limit = lengths[:, None] + 1 + jnp.arange(step_count, dtype=jnp.int32)[None, :]
    usable = slot_positions[:, None, None, :] < step_limit[:, :, None, None]
    masked = jnp.where(usable, scores, large_negative)
    local_peak = jnp.max(masked, axis=-1)
    weights = jnp.where(usable, jnp.exp(masked - local_peak[..., None]), 0.0).astype(jnp.bfloat16)
    numerator = jnp.einsum(
        "bthj,bjl->bthl", weights, key_rows[:, :, :LATENT], preferred_element_type=jnp.float32
    )
    weight_sum = jnp.sum(weights.astype(jnp.float32), axis=-1)
    latent_rows = LATENT // members

    def combine(earlier, later):
        joint = jnp.maximum(earlier[0], later[0])
        early_factor = jnp.exp(earlier[0] - joint)
        late_factor = jnp.exp(later[0] - joint)
        return (
            joint,
            early_factor * earlier[1] + late_factor * later[1],
            early_factor[..., None] * earlier[2] + late_factor[..., None] * later[2],
        )

    merged = combined_all((local_peak, weight_sum, numerator), "context", combine)
    total_all = merged[1]
    own_rows = lax.dynamic_slice_in_dim(merged[2], member_index * latent_rows, latent_rows, 3)
    latent_out = (own_rows / total_all[..., None]).astype(jnp.bfloat16)
    value_terms = jnp.einsum(
        "bthl,hlv->bthv", latent_out, w_value, preferred_element_type=jnp.float32
    )
    head_values = lax.psum(value_terms, "context").astype(jnp.bfloat16)
    flattened = head_values.reshape(
        request_count * step_count, head_values.shape[2] * head_values.shape[3]
    )
    column_terms = jnp.dot(flattened, w_out, preferred_element_type=jnp.float32)
    attn_out = lax.psum_scatter(column_terms, "tensor", scatter_dimension=1, tiled=True).astype(
        jnp.bfloat16
    )
    return (new_cache, attn_out.reshape(request_count, step_count, attn_out.shape[1]))


def solution(mesh):
    placed = (
        P("context", "dp", None, None),
        P("context", "dp", None, None),
        P("dp"),
        P("dp", None),
        P("dp", None, None),
        P("dp", None, "tensor", None),
        P("tensor", "context", None),
        P("tensor", "context"),
    )
    return jax.shard_map(
        body,
        mesh=mesh,
        in_specs=placed,
        out_specs=(P("context", "dp", None, None), P("dp", None, ("context", "tensor"))),
        check_vma=False,
    )
```

profile of v0, /device:TPU:1, one launch (start us, length us, event | category | flops | bytes accessed | tf_op | source)
XLA Modules:
  0.0 404.5 jit_solution(15625536993067821785)
XLA Ops:
  7.2 5.0 %collective-permute-start = (bf16[1,4,256,576]{2,3,1,0:T(8,128)(2,1)}, bf16[1,4,256,576]{2,3,1,0:T(8,128)(2,1)S(1)}, u32[]{:S(2)}, u32[]{:S(2)}) collective-permute-start(bf16[1,4,256,576]{2,3,1,0:T(8,128)(2,1)} %param.11), channel_id=1, source_target_pairs={{60,0},{0,4},{4,8},{8,12},{12,16},{16,20},{20,24},{24,28},{28,32},... | collective-permute-start | bytes 3538952 | tf_op jit(solution)/shard_map/ppermute | solution.py:16
  12.2 2.4 copy.26
  14.8 31.0 %collective-permute-done = bf16[1,4,256,576]{2,3,1,0:T(8,128)(2,1)S(1)} collective-permute-done((bf16[1,4,256,576]{2,3,1,0:T(8,128)(2,1)}, bf16[1,4,256,576]{2,3,1,0:T(8,128)(2,1)S(1)}, u32[]{:S(2)}, u32[]{:S(2)}) %collective-permute-start) | collective-permute-done | bytes 1179680 | tf_op jit(solution)/shard_map/ppermute | solution.py:16
  47.2 1.9 broadcast_select_fusion
  52.5 51.6 %collective-permute-done.1 = bf16[1,4,256,576]{2,3,1,0:T(8,128)(2,1)} collective-permute-done((bf16[1,4,256,576]{2,3,1,0:T(8,128)(2,1)}, bf16[1,4,256,576]{2,3,1,0:T(8,128)(2,1)}, u32[]{:S(2)}, u32[]{:S(2)}) %collective-permute-start.1) | collective-permute-done | bytes 1179680 | tf_op jit(solution)/shard_map/ppermute | solution.py:16
  104.1 2.4 copy.28
  106.5 1.9 broadcast_select_fusion.1
  109.8 4.2 %collective-permute-start.2 = (bf16[1,4,256,576]{2,3,1,0:T(8,128)(2,1)}, bf16[1,4,256,576]{2,3,1,0:T(8,128)(2,1)}, u32[]{:S(2)}, u32[]{:S(2)}) collective-permute-start(bf16[1,4,256,576]{2,3,1,0:T(8,128)(2,1)} %copy.29), channel_id=1, source_target_pairs={{48,0},{52,4},{56,8},{60,12},{0,16},{4,20},{8,24},{12,28},{16,32},... | collective-permute-start | bytes 3538952 | tf_op jit(solution)/shard_map/ppermute | solution.py:16
  114.0 2.5 copy.33
  116.8 43.9 %collective-permute-done.2 = bf16[1,4,256,576]{2,3,1,0:T(8,128)(2,1)} collective-permute-done((bf16[1,4,256,576]{2,3,1,0:T(8,128)(2,1)}, bf16[1,4,256,576]{2,3,1,0:T(8,128)(2,1)}, u32[]{:S(2)}, u32[]{:S(2)}) %collective-permute-start.2) | collective-permute-done | bytes 1179680 | tf_op jit(solution)/shard_map/ppermute | solution.py:16
  160.7 2.4 copy.30
  163.1 1.9 broadcast_select_fusion.2
  166.5 9.0 %collective-permute-start.3 = (bf16[1,4,256,576]{2,3,1,0:T(8,128)(2,1)}, bf16[1,4,256,576]{2,3,1,0:T(8,128)(2,1)}, u32[]{:S(2)}, u32[]{:S(2)}) collective-permute-start(bf16[1,4,256,576]{2,3,1,0:T(8,128)(2,1)} %copy.31), channel_id=1, source_target_pairs={{32,0},{36,4},{40,8},{44,12},{48,16},{52,20},{56,24},{60,28},{0,32... | collective-permute-start | bytes 3538952 | tf_op jit(solution)/shard_map/ppermute | solution.py:16
  175.8 22.7 %collective-permute-done.3 = bf16[1,4,256,576]{2,3,1,0:T(8,128)(2,1)} collective-permute-done((bf16[1,4,256,576]{2,3,1,0:T(8,128)(2,1)}, bf16[1,4,256,576]{2,3,1,0:T(8,128)(2,1)}, u32[]{:S(2)}, u32[]{:S(2)}) %collective-permute-start.3) | collective-permute-done | bytes 1179680 | tf_op jit(solution)/shard_map/ppermute | solution.py:16
  198.5 2.4 copy.32
  206.0 29.3 %all-gather = f32[64,2,16]{2,1,0:T(2,128)S(1)} all-gather(f32[4,2,16]{2,1,0:T(2,128)S(1)} %get-tuple-element.74), channel_id=2, replica_groups=mesh['dp'=8,'context'=16,'tensor'=4] {'context'}, dimensions={0}, use_global_device_ids=true | all-gather | bytes 8704 | tf_op jit(solution)/shard_map/all_gather | solution.py:20
  235.6 25.4 %all-gather.1 = f32[64,2,16]{2,1,0:T(2,128)S(1)} all-gather(f32[4,2,16]{2,1,0:T(2,128)S(1)} %convert_reduce_fusion), channel_id=3, replica_groups=mesh['dp'=8,'context'=16,'tensor'=4] {'context'}, dimensions={0}, use_global_device_ids=true | all-gather | bytes 8704 | tf_op jit(solution)/shard_map/all_gather | solution.py:20
  260.9 18.2 %all-gather.5.cloned.1.call-done = f32[64,2,16,512]{3,2,1,0:T(8,128)} async-done(((f32[4,2,16,512]{3,2,1,0:T(8,128)}), f32[64,2,16,512]{3,2,1,0:T(8,128)}) %all-gather.5.cloned.1.call-update) | async-done | bytes 4194320 | tf_op jit(solution)/shard_map/all_gather | solution.py:20
  279.2 4.8 %slice.52 = f32[60,2,16,512]{3,2,1,0:T(8,128)} slice(f32[64,2,16,512]{3,2,1,0:T(8,128)} %all-gather.5.cloned.1.call-done), slice={[4:64], [0:2], [0:16], [0:512]} | slice | bytes 7864320 | tf_op jit(solution)/shard_map/slice | solution.py:22
  284.0 16.9 %while.14 = (s32[]{:T(128)}, f32[4,2,16]{2,1,0:T(2,128)S(1)}, f32[4,2,16]{2,1,0:T(2,128)S(1)}, f32[4,2,16,512]{3,2,1,0:T(8,128)S(1)}, f32[15,4,2,16]{3,2,1,0:T(2...) while((s32[]{:T(128)}, f32[4,2,16]{2,1,0:T(2,128)S(1)}, ...), condition=%wide.region_3.4_spmd, body=%wide.region_2.3_spmd.sunk | while | flops 197378 | bytes 791653 | solution.py:23
  301.1 49.3 %psum.7 = bf16[4,2,16,128]{3,0,1,2:T(4,128)(2,1)S(1)} all-reduce(f32[4,2,16,128]{3,0,1,2:T(4,128)S(1)} %convolution_bitcast_fusion.1), channel_id=1, replica_groups=mesh['dp'=8,'context'=16,'tensor'=4] {'context'}, use_global_device_ids=true, to_apply=%region_4.5 | all-reduce | flops 16384 | bytes 98304 | tf_op jit(solution)/shard_map/psum | solution.py:85
  351.8 3.1 fusion.3
  354.8 4.3 %copy.38 = bf16[1,4,512,576]{2,3,1,0:T(8,128)(2,1)} copy(bf16[1,4,512,576]{3,2,1,0:T(8,128)(2,1)} %fusion.3) | data formatting | bytes 4718592
  359.1 37.1 %reduce-scatter.4.cloned.1.call-done = f32[112,8]{1,0:T(8,128)} async-done(((f32[448,8]{1,0:T(8,128)}), f32[112,8]{1,0:T(8,128)}) %reduce-scatter.4.cloned.1.call-update) | async-done | bytes 3600
  (89 shorter events, 33.2 us)
Async XLA Ops:
  7.2 343.3 %copy-start = (bf16[2048,448]{0,1:T(8,128)(2,1)S(1)}, bf16[2048,448]{0,1:T(8,128)(2,1)}, u32[]{:S(2)}) copy-start(bf16[2048,448]{0,1:T(8,128)(2,1)} %param.17) | copy-start | bytes 5505028
  7.2 7.4 %copy-start.9 = (s32[4,16]{1,0:T(4,128)S(1)}, s32[4,16]{1,0:T(4,128)}, u32[]{:S(2)}) copy-start(s32[4,16]{1,0:T(4,128)} %param.13) | copy-start | bytes 772
  7.2 272.0 %all-gather.5.cloned.1.call-start = ((), (), s32[]{:S(2)}) async-start(), calls=%async_computation.1 | async-start | bytes 4456448 | tf_op jit(solution)/shard_map/all_gather | solution.py:20
  7.2 38.5 %collective-permute-start = (bf16[1,4,256,576]{2,3,1,0:T(8,128)(2,1)}, bf16[1,4,256,576]{2,3,1,0:T(8,128)(2,1)S(1)}, u32[]{:S(2)}, u32[]{:S(2)}) collective-permute-start(bf16[1,4,256,576]{2,3,1,0:T(8,128)(2,1)} %param.11), channel_id=1, source_target_pairs={{60,0},{0,4},{4,8},{8,12},{12,16},{16,20},{20,24},{24,28},{28,32},... | collective-permute-start | bytes 3538952 | tf_op jit(solution)/shard_map/ppermute | solution.py:16
  49.1 57.3 %copy-start.2 = (bf16[1,4,256,576]{3,2,1,0:T(8,128)(2,1)}, bf16[1,4,256,576]{3,2,1,0:T(8,128)(2,1)S(1)}, u32[]{:S(2)}) copy-start(bf16[1,4,256,576]{3,2,1,0:T(8,128)(2,1)S(1)} %broadcast_select_fusion) | copy-start | bytes 3538948
  50.6 53.5 %collective-permute-start.1 = (bf16[1,4,256,576]{2,3,1,0:T(8,128)(2,1)}, bf16[1,4,256,576]{2,3,1,0:T(8,128)(2,1)}, u32[]{:S(2)}, u32[]{:S(2)}) collective-permute-start(bf16[1,4,256,576]{2,3,1,0:T(8,128)(2,1)} %copy.27), channel_id=1, source_target_pairs={{56,0},{60,4},{0,8},{4,12},{8,16},{12,20},{16,24},{20,28},{24,32},... | collective-permute-start | bytes 3538952 | tf_op jit(solution)/shard_map/ppermute | solution.py:16
  108.4 8.1 %copy-start.1 = (bf16[1,4,256,576]{3,2,1,0:T(8,128)(2,1)}, bf16[1,4,256,576]{3,2,1,0:T(8,128)(2,1)S(1)}, u32[]{:S(2)}) copy-start(bf16[1,4,256,576]{3,2,1,0:T(8,128)(2,1)S(1)} %broadcast_select_fusion.1) | copy-start | bytes 3538948
  109.8 6.8 %copy-start.10 = (s32[4]{0:T(128)S(1)}, s32[4]{0:T(128)}, u32[]{:S(2)}) copy-start(s32[4]{0:T(128)} %param.12) | copy-start | bytes 52
  109.8 50.9 %collective-permute-start.2 = (bf16[1,4,256,576]{2,3,1,0:T(8,128)(2,1)}, bf16[1,4,256,576]{2,3,1,0:T(8,128)(2,1)}, u32[]{:S(2)}, u32[]{:S(2)}) collective-permute-start(bf16[1,4,256,576]{2,3,1,0:T(8,128)(2,1)} %copy.29), channel_id=1, source_target_pairs={{48,0},{52,4},{56,8},{60,12},{0,16},{4,20},{8,24},{12,28},{16,32},... | collective-permute-start | bytes 3538952 | tf_op jit(solution)/shard_map/ppermute | solution.py:16
  165.1 10.7 %copy-start.8 = (bf16[4,2,576]{2,1,0:T(2,128)(2,1)S(1)}, bf16[4,2,576]{2,1,0:T(2,128)(2,1)}, u32[]{:S(2)}) copy-start(bf16[4,2,576]{2,1,0:T(2,128)(2,1)} %param.14) | copy-start | bytes 27652
  166.5 32.0 %collective-permute-start.3 = (bf16[1,4,256,576]{2,3,1,0:T(8,128)(2,1)}, bf16[1,4,256,576]{2,3,1,0:T(8,128)(2,1)}, u32[]{:S(2)}, u32[]{:S(2)}) collective-permute-start(bf16[1,4,256,576]{2,3,1,0:T(8,128)(2,1)} %copy.31), channel_id=1, source_target_pairs={{32,0},{36,4},{40,8},{44,12},{48,16},{52,20},{56,24},{60,28},{0,32... | collective-permute-start | bytes 3538952 | tf_op jit(solution)/shard_map/ppermute | solution.py:16
  200.9 1.7 copy-start.3
  202.5 1.1 copy-start.5
  202.6 1.1 copy-start.6
  206.0 190.3 %reduce-scatter.4.cloned.1.call-start = ((), (), s32[]{:S(2)}) async-start(), calls=%async_computation.2 | async-start | bytes 286720
  279.2 4.8 %slice-start = ((f32[64,2,16,512]{3,2,1,0:T(8,128)}), f32[4,2,16,512]{3,2,1,0:T(8,128)S(1)}, s32[]{:S(2)}) async-start(f32[64,2,16,512]{3,2,1,0:T(8,128)} %all-gather.5.cloned.1.call-done), calls=%async_computation.3 | async-start | bytes 524288 | tf_op jit(solution)/shard_map/slice | solution.py:21
  284.0 17.0 %copy-start.7 = (bf16[16,32,128]{2,1,0:T(8,128)(2,1)S(1)}, bf16[16,32,128]{2,1,0:T(8,128)(2,1)}, u32[]{:S(2)}) copy-start(bf16[16,32,128]{2,1,0:T(8,128)(2,1)} %param.16) | copy-start | bytes 393220
  301.1 50.6 %copy-start.4 = (bf16[1,4,256,576]{3,2,1,0:T(8,128)(2,1)S(1)}, bf16[1,4,256,576]{3,2,1,0:T(8,128)(2,1)}, u32[]{:S(2)}) copy-start(bf16[1,4,256,576]{3,2,1,0:T(8,128)(2,1)} %copy.33) | copy-start | bytes 3538948
Sparse Core Ops, SparseCore 0:
  206.1 73.0 all-gather.4
  351.9 44.2 reduce-scatter.3
where the time goes:
time: 407 us; the launch traced here: 405 us
  waiting for transfers between devices  205 us (50%)
  blocking collectives  104 us (26%)
  other arithmetic  28.9 us (7%)
  local copies, waits for them, and re-layouts  28.7 us (7%)
  starting transfers between devices  20.2 us (5%)
  between operations  14.3 us (4%)
    ppermute x4, waiting for transfers between devices, passed_along(): return lax.ppermute(block, axis, route)  149 us
    all_gather x2, blocking collectives, combined_all(): pieces = jax.tree.map(lambda part: lax.all_gather(part, axis), value)  54.7 us
    psum x1, blocking collectives, body(): head_values = lax.psum(value_terms, 'context').astype(jnp.bfloat16)  49.3 us
    unnamed x3, waiting for transfers between devices  37.1 us
    ppermute x4, starting transfers between devices, passed_along(): return lax.ppermute(block, axis, route)  20.1 us
    all_gather x1, waiting for transfers between devices, combined_all(): pieces = jax.tree.map(lambda part: lax.all_gather(part, axis), value)  18.2 us
    add x15, other arithmetic, combine(): early_factor[..., None] * earlier[2] + late_factor[..., None] * later[2]  16.1 us
    unnamed x27, local copies, waits for them, and re-layouts  10.9 us
  transfers between devices with their start and end apart: 6, of which 6 were waited for; matrix products, arithmetic and copies ran while one was open for 3% of the time, Pallas kernels for 0%

commit v1 on v0

v1 whole, which is shorter than its diff:
```python
import jax
import jax.numpy as jnp
from jax import lax
from jax.experimental import pallas as pl
from jax.experimental.pallas import tpu as pltpu
from jax.sharding import PartitionSpec as P

REQ = 4
STEPS = 2
HEADS = 16
LATENT = 512
WIDTH = 576
SLICE = 256
MEMBERS = 16
TENSOR = 4
LANES = 128
CHUNK = WIDTH * SLICE // (MEMBERS * LANES)
VROWS = LATENT // MEMBERS
NROWS = 48
OUTC = 112

softmax_scale = 0.07216878364870322
large_negative = -1e30

f32 = jnp.float32
bf16 = jnp.bfloat16

VMEM = pl.BlockSpec(memory_space=pltpu.VMEM)
SMEM = pl.BlockSpec(memory_space=pltpu.SMEM)
ANY = pl.BlockSpec(memory_space=pl.ANY)


def nt_dot(a, b):
    return lax.dot_general(a, b, (((1,), (1,)), ((), ())), preferred_element_type=f32)


def with_new_entries(block, entries, length, member):
    first = (MEMBERS + member) * SLICE
    slot = lax.broadcasted_iota(jnp.int32, (STEPS, SLICE), 1)
    step = lax.broadcasted_iota(jnp.int32, (STEPS, SLICE), 0)
    hit = (slot + first == length + step).astype(f32)
    placed = lax.dot_general(
        entries, hit.astype(bf16), (((0,), (0,)), ((), ())), preferred_element_type=f32
    )
    taken = jnp.max(hit, axis=0, keepdims=True) > 0.5
    return jnp.where(taken, placed, block.astype(f32)).astype(bf16)


def pack_kernel(lengths, entries, leaving, w_value, out, block, sem):
    tensor = lax.axis_index("tensor")
    member = lax.axis_index("context")
    copy = pltpu.make_async_copy(leaving.at[tensor], block, sem)
    copy.start()
    out[:, 0:VROWS, :] = w_value[...]
    copy.wait()
    updated = with_new_entries(block[...], entries[tensor], lengths[tensor], member)
    for c in range(MEMBERS):
        row, lane = (c % 8) * CHUNK, (c // 8) * LANES
        out[c, VROWS : VROWS + CHUNK, :] = updated[row : row + CHUNK, lane : lane + LANES]


def attention_kernel(lengths, entries, queries, staying, leaving, out, cache, sem):
    member = lax.axis_index("context")
    copy = pltpu.make_async_copy(staying, cache.at[:, :, 0:SLICE], sem)
    copy.start()
    row = lax.broadcasted_iota(jnp.int32, (STEPS * HEADS, SLICE), 0)
    slot = lax.broadcasted_iota(jnp.int32, (STEPS * HEADS, SLICE), 1)
    step = (row >= HEADS).astype(jnp.int32)
    lane = lax.broadcasted_iota(jnp.int32, (STEPS * HEADS, LANES), 1)
    parts = []
    for b in range(REQ):
        q = queries[b]
        kept = staying[b]
        moved = with_new_entries(leaving[b], entries[b], lengths[b], member)
        limit = lengths[b] + 1 + step
        use_kept = slot + member * SLICE < limit
        use_moved = slot + (MEMBERS + member) * SLICE < limit
        kept_scores = jnp.dot(q, kept, preferred_element_type=f32) * softmax_scale
        moved_scores = jnp.dot(q, moved, preferred_element_type=f32) * softmax_scale
        kept_scores = jnp.where(use_kept, kept_scores, large_negative)
        moved_scores = jnp.where(use_moved, moved_scores, large_negative)
        peak = jnp.maximum(
            jnp.max(kept_scores, axis=1, keepdims=True),
            jnp.max(moved_scores, axis=1, keepdims=True),
        )
        peak = peak.astype(bf16).astype(f32)
        kept_w = jnp.where(use_kept, jnp.exp(kept_scores - peak), 0.0).astype(bf16)
        moved_w = jnp.where(use_moved, jnp.exp(moved_scores - peak), 0.0).astype(bf16)
        numerator = nt_dot(kept_w, kept[:LATENT]) + nt_dot(moved_w, moved[:LATENT])
        total = jnp.sum(kept_w.astype(f32) + moved_w.astype(f32), axis=1, keepdims=True)
        high = total.astype(bf16).astype(f32)
        stats = jnp.where(
            lane == 0, peak, jnp.where(lane == 1, high, jnp.where(lane == 2, total - high, 0.0))
        )
        both = jnp.concatenate([numerator, stats], axis=1)
        parts += [both[:HEADS], both[HEADS:]]
    by_head = jnp.transpose(jnp.stack(parts), (1, 0, 2))
    tiles = [by_head[:, :, i * LANES : (i + 1) * LANES] for i in range(5)]
    tiles.append(jnp.zeros_like(tiles[0]))
    for i in range(3):
        pair = jnp.concatenate([tiles[2 * i], tiles[2 * i + 1]], axis=1)
        out[:, 16 * i : 16 * (i + 1), :] = pair.astype(bf16)
    copy.wait()


def roll_kernel(pairing, chunks, partials, out):
    offset = pairing[lax.axis_index("tensor"), 0]
    out[:, 0:NROWS, :] = partials[...]
    for r in range(MEMBERS):
        source = lax.rem(r + MEMBERS - offset, MEMBERS)
        out[r, NROWS : NROWS + CHUNK, :] = chunks[source, VROWS : VROWS + CHUNK, :]


def merge_kernel(partials, w_value, out):
    rows = partials[...].astype(f32)
    stats = rows[:, 32:40, :]
    peak = stats[:, :, 0:1]
    top = jnp.max(peak, axis=0, keepdims=True)
    factor = jnp.exp(peak - top)
    total = jnp.sum(factor * (stats[:, :, 1:2] + stats[:, :, 2:3]), axis=0)
    weights = w_value[...].reshape(LATENT, LANES)
    values = jnp.zeros((REQ * STEPS, LANES), f32)
    for i in range(4):
        numerator = jnp.sum(factor * rows[:, 8 * i : 8 * (i + 1), :], axis=0)
        latent = (numerator / total).astype(bf16)
        values += jnp.dot(
            latent, weights[i * LANES : (i + 1) * LANES], preferred_element_type=f32
        )
    out[...] = jnp.broadcast_to(values.astype(bf16)[None], out.shape)


def project_kernel(values, w_out, out):
    flat = jnp.concatenate([values[h] for h in range(HEADS)], axis=1)
    for i in range(TENSOR):
        out[i] = nt_dot(flat, w_out[OUTC * i : OUTC * (i + 1), :])


def fill_kernel(cache_in, received, cache, sems):
    copies = []
    for b in range(REQ):
        for k in range(2):
            lane = SLICE + k * LANES
            copies.append(
                pltpu.make_async_copy(
                    received.at[b, k], cache.at[b, :, lane : lane + LANES], sems.at[b, k]
                )
            )
    for copy in copies:
        copy.start()
    for copy in copies:
        copy.wait()


def body(staying_cache, leaving_cache, lengths, pairing, new_entries, queries, w_value, w_out):
    staying = jnp.swapaxes(staying_cache[0], 1, 2)
    leaving = jnp.swapaxes(leaving_cache[0], 1, 2)
    q = queries.reshape(REQ, STEPS * HEADS, WIDTH)

    first = pl.pallas_call(
        pack_kernel,
        out_shape=jax.ShapeDtypeStruct((MEMBERS, VROWS + CHUNK, LANES), bf16),
        in_specs=[SMEM, VMEM, ANY, VMEM],
        out_specs=VMEM,
        scratch_shapes=[pltpu.VMEM((WIDTH, SLICE), bf16), pltpu.SemaphoreType.DMA],
        name="pack",
    )(lengths, new_entries, leaving, w_value)
    chunks = lax.all_to_all(first, "context", 0, 0)

    partials, cache = pl.pallas_call(
        attention_kernel,
        out_shape=(
            jax.ShapeDtypeStruct((MEMBERS, NROWS, LANES), bf16),
            jax.ShapeDtypeStruct((REQ, WIDTH, 2 * SLICE), bf16),
        ),
        in_specs=[SMEM, VMEM, VMEM, VMEM, VMEM],
        out_specs=(VMEM, ANY),
        scratch_shapes=[pltpu.SemaphoreType.DMA],
        cost_estimate=pl.CostEstimate(
            flops=300_000_000, bytes_accessed=8_000_000, transcendentals=65536
        ),
        name="attend",
    )(lengths, new_entries, q, staying, leaving)

    second = pl.pallas_call(
        roll_kernel,
        out_shape=jax.ShapeDtypeStruct((MEMBERS, NROWS + CHUNK, LANES), bf16),
        in_specs=[SMEM, VMEM, VMEM],
        out_specs=VMEM,
        name="roll",
    )(pairing, chunks, partials)
    arrived = lax.all_to_all(second, "context", 0, 0)

    received = lax.all_gather(arrived[:, NROWS:, :], "tensor")
    received = received.reshape(REQ, 2, WIDTH, LANES)

    values = pl.pallas_call(
        merge_kernel,
        out_shape=jax.ShapeDtypeStruct((MEMBERS, REQ * STEPS, LANES), bf16),
        grid=(1,),
        in_specs=[
            pl.BlockSpec((MEMBERS, NROWS, LANES), lambda i: (0, 0, 0)),
            pl.BlockSpec((MEMBERS, VROWS, LANES), lambda i: (0, 0, 0)),
        ],
        out_specs=pl.BlockSpec((MEMBERS, REQ * STEPS, LANES), lambda i: (0, 0, 0)),
        name="merge",
    )(arrived, chunks)
    all_values = lax.all_to_all(values, "context", 0, 0)

    columns = pl.pallas_call(
        project_kernel,
        out_shape=jax.ShapeDtypeStruct((TENSOR, REQ * STEPS, OUTC), f32),
        in_specs=[VMEM, VMEM],
        out_specs=VMEM,
        name="project",
    )(all_values, w_out.T)
    terms = lax.all_to_all(columns, "tensor", 0, 0)
    attn_out = jnp.sum(terms, axis=0).astype(bf16).reshape(REQ, STEPS, OUTC)

    cache = pl.pallas_call(
        fill_kernel,
        out_shape=jax.ShapeDtypeStruct((REQ, WIDTH, 2 * SLICE), bf16),
        in_specs=[ANY, ANY],
        out_specs=ANY,
        scratch_shapes=[pltpu.SemaphoreType.DMA((REQ, 2))],
        input_output_aliases={0: 0},
        name="fill",
    )(cache, received)
    return (jnp.swapaxes(cache, 1, 2)[None], attn_out)


def solution(mesh):
    placed = (
        P("context", "dp", None, None),
        P("context", "dp", None, None),
        P("dp"),
        P("dp", None),
        P("dp", None, None),
        P("dp", None, "tensor", None),
        P("tensor", "context", None),
        P("tensor", "context"),
    )
    return jax.shard_map(
        body,
        mesh=mesh,
        in_specs=placed,
        out_specs=(P("context", "dp", None, None), P("dp", None, ("context", "tensor"))),
        check_vma=False,
    )
```

time: 407 us -> 140 us (0.34)
  waiting for transfers between devices: 205 us -> 10.4 us
  blocking collectives: 104 us -> 49.8 us
  Pallas kernels: 0 us -> 51.3 us
  other arithmetic: 28.9 us -> 0.59 us
  local copies, waits for them, and re-layouts: 28.7 us -> 1.64 us
  starting transfers between devices: 20.2 us -> 12 us
    ppermute x4 -> x0, waiting for transfers between devices: 149 us -> none  [passed_along(): return lax.ppermute(block, axis, route)]
    all_gather x2 -> x0, blocking collectives: 54.7 us -> none  [combined_all(): pieces = jax.tree.map(lambda part: lax.all_gather(part, axis), value)]
    pallas_call x0 -> x6, Pallas kernels: none -> 51.3 us  [the longest x1 36.9 us: body(): pl.pallas_call(fill_kernel, out_shape=jax.ShapeDtypeStruct((REQ, WIDTH, 2...]
    all_to_all x0 -> x3, blocking collectives: none -> 49.8 us  [the longest x1 20.5 us: body(): arrived = lax.all_to_all(second, 'context', 0, 0)]
    psum x1 -> x0, blocking collectives: 49.3 us -> none  [body(): head_values = lax.psum(value_terms, 'context').astype(jnp.bfloat16)]
    unnamed x3 -> x1, waiting for transfers between devices: 37.1 us -> 0.02 us
    ppermute x4 -> x0, starting transfers between devices: 20.1 us -> none  [passed_along(): return lax.ppermute(block, axis, route)]
    add x34 -> x0, other arithmetic: 16.7 us -> none  [the longest x15 16.1 us: combine(): early_factor[..., None] * earlier[2] + late_factor[..., None] * later[2]]
  transfers between devices with their start and end apart: 6 -> 2, of which waited for: 6 -> 2; matrix products, arithmetic and copies ran while one was open for 3% -> 0% of each run, Pallas kernels for 0% -> 7%
where the time goes in v1:
time: 140 us
  Pallas kernels  51.3 us (37%)
  blocking collectives  49.8 us (36%)
  between operations  14.1 us (10%)
  starting transfers between devices  12 us (9%)
  waiting for transfers between devices  10.4 us (7%)
  local copies, waits for them, and re-layouts  1.64 us (1%)
    pallas_call x1, Pallas kernels, body(): pl.pallas_call(fill_kernel, out_shape=jax.ShapeDtypeStruct((REQ, WIDTH, 2...  36.9 us
    all_to_all x1, blocking collectives, body(): arrived = lax.all_to_all(second, 'context', 0, 0)  20.5 us
    all_to_all x1, blocking collectives, body(): all_values = lax.all_to_all(values, 'context', 0, 0)  15.7 us
    all_to_all x1, blocking collectives, body(): terms = lax.all_to_all(columns, 'tensor', 0, 0)  13.7 us
    all_to_all x1, starting transfers between devices, body(): chunks = lax.all_to_all(first, 'context', 0, 0)  12 us
    all_gather x1, waiting for transfers between devices, body(): received = lax.all_gather(arrived[:, NROWS:, :], 'tensor')  5.74 us
    pallas_call x1, Pallas kernels, body(): pl.pallas_call(attention_kernel, out_shape=(jax.ShapeDtypeStruct((MEMBERS...  4.89 us
    all_to_all x1, waiting for transfers between devices, body(): chunks = lax.all_to_all(first, 'context', 0, 0)  4.64 us
  transfers between devices with their start and end apart: 2, of which 2 were waited for; matrix products, arithmetic and copies ran while one was open for 0% of the time, Pallas kernels for 7%

profile of v1, /device:TPU:1, one launch (start us, length us, event | category | flops | bytes accessed | tf_op | source)
XLA Modules:
  0.0 139.9 jit_solution(11822613605346209110)
XLA Ops:
  7.2 2.9 %pack.1 = bf16[16,104,128]{2,1,0:T(8,128)(2,1)} custom-call(s32[4]{0:T(128)} %lengths.3, bf16[4,2,576]{2,1,0:T(2,128)(2,1)} %entries.3, bf16[4,576,256]{2,1,0:T(8,128)(2,1)} %bitcast.13, bf16[16,32,128]{2,1,0:T(8,128)(2,1)} %w_value.1), custom_call_target="tpu_custom_call" | custom-call | tf_op jit(solution)/shard_map/pack/pallas_call | solution.py:159
  10.1 12.0 %all-to-all-start = ((bf16[16,104,128]{2,1,0:T(8,128)(2,1)}), bf16[16,104,128]{2,1,0:T(8,128)(2,1)S(1)}, u32[]{:S(2)}, u32[]{:S(2)}) async-start(bf16[16,104,128]{2,1,0:T(8,128)(2,1)} %pack.1), calls=%async_computation | async-start | bytes 851968 | tf_op jit(solution)/shard_map/all_to_all | solution.py:167
  22.1 0.0 all-gather.3.cloned.1.call-start
  22.2 4.9 %attend.1 = (bf16[16,48,128]{2,1,0:T(8,128)(2,1)}, bf16[4,576,512]{2,1,0:T(8,128)(2,1)}) custom-call(s32[4]{0:T(128)} %lengths.3, bf16[4,2,576]{2,1,0:T(2,128)(2,1)} %entries.3, bf16[4,32,576]{2,1,0:T(8,128)(2,1)} %bitcast.19, bf16[4,576,256]{2,1,0:T(8,128)(2,1)} %bitcast.17, bf16[4,576,256]{2,1,0:T(8,128)(2,1)} %bitcast.14), custom_call_target="tpu_custom_call" | custom-call | flops 300000000 | bytes 8000000 | tf_op jit(solution)/shard_map/attend/pallas_call | solution.py:169
  27.1 4.6 %all-to-all-done.chunks.w_value = bf16[16,104,128]{2,1,0:T(8,128)(2,1)S(1)} async-done(((bf16[16,104,128]{2,1,0:T(8,128)(2,1)}), bf16[16,104,128]{2,1,0:T(8,128)(2,1)S(1)}, u32[]{:S(2)}, u32[]{:S(2)}) %all-to-all-start) | async-done | bytes 426016 | tf_op jit(solution)/shard_map/all_to_all | solution.py:167
  31.7 0.0 copy-start
  31.7 0.8 copy-done
  32.5 1.9 %roll.1 = bf16[16,120,128]{2,1,0:T(8,128)(2,1)} custom-call(s32[4,16]{1,0:T(4,128)} %pairing.1, bf16[16,104,128]{2,1,0:T(8,128)(2,1)} %copy-done, bf16[16,48,128]{2,1,0:T(8,128)(2,1)} %get-tuple-element.5.partials), custom_call_target="tpu_custom_call" | custom-call | tf_op jit(solution)/shard_map/roll/pallas_call | solution.py:184
  34.4 20.5 %all_to_all.20.partials = bf16[16,120,128]{2,1,0:T(8,128)(2,1)S(1)} all-to-all(bf16[16,120,128]{2,1,0:T(8,128)(2,1)} %roll.1), channel_id=1, replica_groups=mesh['dp'=8,'context'=16,'tensor'=4] {'context'}, dimensions={0} | all-to-all | bytes 983040 | tf_op jit(solution)/shard_map/all_to_all | solution.py:191
  54.8 0.0 copy-start.1
  54.8 0.8 slice.4
  55.6 0.0 all-gather.3.cloned.1.call-update
  55.7 0.1 copy-done.1
  55.8 2.0 %merge.1 = bf16[16,8,128]{2,1,0:T(8,128)(2,1)} custom-call(bf16[16,120,128]{2,1,0:T(8,128)(2,1)} %copy-done.1, bf16[16,104,128]{2,1,0:T(8,128)(2,1)} %copy-done), custom_call_target="tpu_custom_call" | custom-call | tf_op jit(solution)/shard_map/merge/pallas_call | solution.py:196
  57.7 15.7 %all_to_all.21.values = bf16[16,8,128]{2,1,0:T(8,128)(2,1)} all-to-all(bf16[16,8,128]{2,1,0:T(8,128)(2,1)} %merge.1), channel_id=1, replica_groups=mesh['dp'=8,'context'=16,'tensor'=4] {'context'}, dimensions={0} | all-to-all | bytes 65536 | tf_op jit(solution)/shard_map/all_to_all | solution.py:207
  73.4 2.7 %project.1 = f32[4,8,112]{2,1,0:T(8,128)} custom-call(bf16[16,8,128]{2,1,0:T(8,128)(2,1)} %all_to_all.21.values, bf16[448,2048]{1,0:T(8,128)(2,1)} %bitcast.16), custom_call_target="tpu_custom_call" | custom-call | tf_op jit(solution)/shard_map/project/pallas_call | solution.py:209
  76.1 13.7 %all_to_all.22 = f32[4,8,112]{2,1,0:T(8,128)S(1)} all-to-all(f32[4,8,112]{2,1,0:T(8,128)} %project.1), channel_id=1, replica_groups=mesh['dp'=8,'context'=16,'tensor'=4] {'tensor'}, dimensions={0} | all-to-all | bytes 28672 | tf_op jit(solution)/shard_map/all_to_all | solution.py:216
  89.8 0.6 reduce_sum.9
  90.4 5.7 %all-gather.3.cloned.1.call-done = bf16[64,72,128]{2,1,0:T(8,128)(2,1)} async-done(((bf16[16,72,128]{2,1,0:T(8,128)(2,1)}), bf16[64,72,128]{2,1,0:T(8,128)(2,1)}) %all-gather.3.cloned.1.call-update) | async-done | bytes 1179664 | tf_op jit(solution)/shard_map/all_gather | solution.py:193
  96.1 36.9 %fill.1 = bf16[4,576,512]{2,1,0:T(8,128)(2,1)} custom-call(bf16[4,576,512]{2,1,0:T(8,128)(2,1)} %get-tuple-element.4.cache_in, bf16[4,2,576,128]{3,2,1,0:T(8,128)(2,1)} %bitcast.18), custom_call_target="tpu_custom_call", output_to_operand_aliasing={{}: (0, {})} | custom-call | tf_op jit(solution)/shard_map/fill/pallas_call | solution.py:219
Async XLA Ops:
  10.1 21.6 %all-to-all-start = ((bf16[16,104,128]{2,1,0:T(8,128)(2,1)}), bf16[16,104,128]{2,1,0:T(8,128)(2,1)S(1)}, u32[]{:S(2)}, u32[]{:S(2)}) async-start(bf16[16,104,128]{2,1,0:T(8,128)(2,1)} %pack.1), calls=%async_computation | async-start | bytes 851968 | tf_op jit(solution)/shard_map/all_to_all | solution.py:167
  22.1 74.0 %all-gather.3.cloned.1.call-start = ((), (), s32[]{:S(2)}) async-start(), calls=%async_computation.4 | async-start | bytes 1474560 | tf_op jit(solution)/shard_map/all_gather | solution.py:193
  31.7 0.8 copy-start
  54.8 0.9 copy-start.1
Sparse Core Ops, SparseCore 0:
  55.8 40.2 all-gather.2

commit v2 on v1

--- a/solution.py
+++ b/solution.py
@@ -46,23 +46,15 @@
     return jnp.where(taken, placed, block.astype(f32)).astype(bf16)
 
 
-def pack_kernel(lengths, entries, leaving, w_value, out, block, sem):
+def update_kernel(lengths, entries, leaving, out):
     tensor = lax.axis_index("tensor")
     member = lax.axis_index("context")
-    copy = pltpu.make_async_copy(leaving.at[tensor], block, sem)
-    copy.start()
-    out[:, 0:VROWS, :] = w_value[...]
-    copy.wait()
-    updated = with_new_entries(block[...], entries[tensor], lengths[tensor], member)
-    for c in range(MEMBERS):
-        row, lane = (c % 8) * CHUNK, (c // 8) * LANES
-        out[c, VROWS : VROWS + CHUNK, :] = updated[row : row + CHUNK, lane : lane + LANES]
-
-
-def attention_kernel(lengths, entries, queries, staying, leaving, out, cache, sem):
+    out[...] = with_new_entries(leaving[0], entries[tensor], lengths[tensor], member)
+
+
+def attention_kernel(lengths, entries, queries, staying, leaving, w_value, out):
     member = lax.axis_index("context")
-    copy = pltpu.make_async_copy(staying, cache.at[:, :, 0:SLICE], sem)
-    copy.start()
+    out[:, NROWS : NROWS + VROWS, :] = w_value[...]
     row = lax.broadcasted_iota(jnp.int32, (STEPS * HEADS, SLICE), 0)
     slot = lax.broadcasted_iota(jnp.int32, (STEPS * HEADS, SLICE), 1)
     step = (row >= HEADS).astype(jnp.int32)
@@ -100,25 +92,16 @@
     for i in range(3):
         pair = jnp.concatenate([tiles[2 * i], tiles[2 * i + 1]], axis=1)
         out[:, 16 * i : 16 * (i + 1), :] = pair.astype(bf16)
-    copy.wait()
-
-
-def roll_kernel(pairing, chunks, partials, out):
-    offset = pairing[lax.axis_index("tensor"), 0]
-    out[:, 0:NROWS, :] = partials[...]
-    for r in range(MEMBERS):
-        source = lax.rem(r + MEMBERS - offset, MEMBERS)
-        out[r, NROWS : NROWS + CHUNK, :] = chunks[source, VROWS : VROWS + CHUNK, :]
-
-
-def merge_kernel(partials, w_value, out):
-    rows = partials[...].astype(f32)
+
+
+def merge_kernel(arrived, out):
+    rows = arrived[:, 0:NROWS, :].astype(f32)
     stats = rows[:, 32:40, :]
     peak = stats[:, :, 0:1]
     top = jnp.max(peak, axis=0, keepdims=True)
     factor = jnp.exp(peak - top)
     total = jnp.sum(factor * (stats[:, :, 1:2] + stats[:, :, 2:3]), axis=0)
-    weights = w_value[...].reshape(LATENT, LANES)
+    weights = arrived[:, NROWS : NROWS + VROWS, :].reshape(LATENT, LANES)
     values = jnp.zeros((REQ * STEPS, LANES), f32)
     for i in range(4):
         numerator = jnp.sum(factor * rows[:, 8 * i : 8 * (i + 1), :], axis=0)
@@ -135,75 +118,75 @@
         out[i] = nt_dot(flat, w_out[OUTC * i : OUTC * (i + 1), :])
 
 
-def fill_kernel(cache_in, received, cache, sems):
-    copies = []
-    for b in range(REQ):
-        for k in range(2):
-            lane = SLICE + k * LANES
-            copies.append(
-                pltpu.make_async_copy(
-                    received.at[b, k], cache.at[b, :, lane : lane + LANES], sems.at[b, k]
-                )
-            )
-    for copy in copies:
-        copy.start()
-    for copy in copies:
-        copy.wait()
+def keep_kernel(staying, columns, cache, sem):
+    copy = pltpu.make_async_copy(staying, cache.at[:, :, 0:SLICE], sem)
+    copy.start()
+    copy.wait()
+
+
+def fill_kernel(cache_in, received, cache, sem):
+    copy = pltpu.make_async_copy(received, cache.at[:, :, SLICE : 2 * SLICE], sem)
+    copy.start()
+    copy.wait()
+
+
+def attend(lengths, entries, queries, staying, leaving, w_value):
+    return pl.pallas_call(
+        attention_kernel,
+        out_shape=jax.ShapeDtypeStruct((MEMBERS, NROWS + VROWS, LANES), bf16),
+        in_specs=[SMEM, VMEM, VMEM, VMEM, VMEM, VMEM],
+        out_specs=VMEM,
+        cost_estimate=pl.CostEstimate(
+            flops=300_000_000, bytes_accessed=4_000_000, transcendentals=65536
+        ),
+        name="attend",
+    )(lengths, entries, queries, staying, leaving, w_value)
+
+
+def exchange(distance):
+    route = [((r - distance) % MEMBERS, r) for r in range(MEMBERS)]
+
+    def branch(block, *operands):
+        moved = lax.ppermute(block, "context", route) if distance else block
+        return moved, lax.all_to_all(attend(*operands), "context", 0, 0)
+
+    return branch
 
 
 def body(staying_cache, leaving_cache, lengths, pairing, new_entries, queries, w_value, w_out):
     staying = jnp.swapaxes(staying_cache[0], 1, 2)
     leaving = jnp.swapaxes(leaving_cache[0], 1, 2)
     q = queries.reshape(REQ, STEPS * HEADS, WIDTH)
-
-    first = pl.pallas_call(
-        pack_kernel,
-        out_shape=jax.ShapeDtypeStruct((MEMBERS, VROWS + CHUNK, LANES), bf16),
-        in_specs=[SMEM, VMEM, ANY, VMEM],
-        out_specs=VMEM,
-        scratch_shapes=[pltpu.VMEM((WIDTH, SLICE), bf16), pltpu.SemaphoreType.DMA],
-        name="pack",
-    )(lengths, new_entries, leaving, w_value)
-    chunks = lax.all_to_all(first, "context", 0, 0)
-
-    partials, cache = pl.pallas_call(
-        attention_kernel,
-        out_shape=(
-            jax.ShapeDtypeStruct((MEMBERS, NROWS, LANES), bf16),
-            jax.ShapeDtypeStruct((REQ, WIDTH, 2 * SLICE), bf16),
-        ),
-        in_specs=[SMEM, VMEM, VMEM, VMEM, VMEM],
-        out_specs=(VMEM, ANY),
-        scratch_shapes=[pltpu.SemaphoreType.DMA],
-        cost_estimate=pl.CostEstimate(
-            flops=300_000_000, bytes_accessed=8_000_000, transcendentals=65536
-        ),
-        name="attend",
-    )(lengths, new_entries, q, staying, leaving)
-
-    second = pl.pallas_call(
-        roll_kernel,
-        out_shape=jax.ShapeDtypeStruct((MEMBERS, NROWS + CHUNK, LANES), bf16),
-        in_specs=[SMEM, VMEM, VMEM],
-        out_specs=VMEM,
-        name="roll",
-    )(pairing, chunks, partials)
-    arrived = lax.all_to_all(second, "context", 0, 0)
-
-    received = lax.all_gather(arrived[:, NROWS:, :], "tensor")
-    received = received.reshape(REQ, 2, WIDTH, LANES)
+    tensor = lax.axis_index("tensor")
+
+    block = pl.pallas_call(
+        update_kernel,
+        out_shape=jax.ShapeDtypeStruct((WIDTH, SLICE), bf16),
+        grid=(1,),
+        in_specs=[
+            SMEM,
+            VMEM,
+            pl.BlockSpec((1, WIDTH, SLICE), lambda i: (lax.axis_index("tensor"), 0, 0)),
+        ],
+        out_specs=VMEM,
+        name="update",
+    )(lengths, new_entries, leaving)
+
+    offset = lax.dynamic_index_in_dim(pairing[:, 0], tensor, 0, False) % MEMBERS
+    moved, arrived = lax.switch(
+        offset,
+        [exchange(d) for d in range(MEMBERS)],
+        block, lengths, new_entries, q, staying, leaving, w_value,
+    )
+    received = lax.all_gather(moved, "tensor")
 
     values = pl.pallas_call(
         merge_kernel,
         out_shape=jax.ShapeDtypeStruct((MEMBERS, REQ * STEPS, LANES), bf16),
-        grid=(1,),
-        in_specs=[
-            pl.BlockSpec((MEMBERS, NROWS, LANES), lambda i: (0, 0, 0)),
-            pl.BlockSpec((MEMBERS, VROWS, LANES), lambda i: (0, 0, 0)),
-        ],
-        out_specs=pl.BlockSpec((MEMBERS, REQ * STEPS, LANES), lambda i: (0, 0, 0)),
+        in_specs=[VMEM],
+        out_specs=VMEM,
         name="merge",
-    )(arrived, chunks)
+    )(arrived)
     all_values = lax.all_to_all(values, "context", 0, 0)
 
     columns = pl.pallas_call(
@@ -217,11 +200,20 @@
     attn_out = jnp.sum(terms, axis=0).astype(bf16).reshape(REQ, STEPS, OUTC)
 
     cache = pl.pallas_call(
+        keep_kernel,
+        out_shape=jax.ShapeDtypeStruct((REQ, WIDTH, 2 * SLICE), bf16),
+        in_specs=[VMEM, ANY],
+        out_specs=ANY,
+        scratch_shapes=[pltpu.SemaphoreType.DMA],
+        cost_estimate=pl.CostEstimate(flops=0, bytes_accessed=8_000_000, transcendentals=0),
+        name="keep",
+    )(staying, columns)
+    cache = pl.pallas_call(
         fill_kernel,
         out_shape=jax.ShapeDtypeStruct((REQ, WIDTH, 2 * SLICE), bf16),
-        in_specs=[ANY, ANY],
+        in_specs=[ANY, VMEM],
         out_specs=ANY,
-        scratch_shapes=[pltpu.SemaphoreType.DMA((REQ, 2))],
+        scratch_shapes=[pltpu.SemaphoreType.DMA],
         input_output_aliases={0: 0},
         name="fill",
     )(cache, received)

time: 140 us -> 108 us (0.77)
  blocking collectives: 49.8 us -> 12.1 us
  Pallas kernels: 51.3 us -> 14.3 us
  waiting for transfers between devices: 10.4 us -> 39.4 us
  starting transfers between devices: 12 us -> 23.3 us
  between operations: 14.1 us -> 16.1 us
    pallas_call x1, Pallas kernels: 36.9 us -> 2.29 us  [body(): pl.pallas_call(fill_kernel, out_shape=jax.ShapeDtypeStruct((REQ, WIDTH, 2...]
    all_to_all x2 -> x0, blocking collectives: 34.2 us -> none  [the longest x1 20.5 us: body(): arrived = lax.all_to_all(second, 'context', 0, 0)]
    ppermute x0 -> x1, waiting for transfers between devices: none -> 21.2 us  [branch(): moved = lax.ppermute(block, 'context', route) if distance else block]
    ppermute x0 -> x1, starting transfers between devices: none -> 8.03 us  [branch(): moved = lax.ppermute(block, 'context', route) if distance else block]
    all_gather x1, waiting for transfers between devices: 5.74 us -> 12 us  [body(): received = lax.all_gather(moved, 'tensor')]
    all_to_all x1, blocking collectives: 15.7 us -> 12.1 us  [body(): all_values = lax.all_to_all(values, 'context', 0, 0)]
    all_to_all x1 -> x2, starting transfers between devices: 12 us -> 15.3 us  [the longest x1 12 us: branch(): return (moved, lax.all_to_all(attend(*operands), 'context', 0, 0))]
    pallas_call x3, Pallas kernels: 9.73 us -> 7.22 us  [the longest x1 4.93 us: attend(): pl.pallas_call(attention_kernel, out_shape=jax.ShapeDtypeStruct((MEMBERS,...]
  transfers between devices with their start and end apart: 2 -> 4, of which waited for: 2 -> 3; matrix products, arithmetic and copies ran while one was open for 0% -> 1% of each run, Pallas kernels for 7% -> 5%
where the time goes in v2:
time: 108 us
  waiting for transfers between devices  39.4 us (36%)
  starting transfers between devices  23.3 us (22%)
  between operations  16.1 us (15%)
  Pallas kernels  14.3 us (13%)
  blocking collectives  12.1 us (11%)
  local copies, waits for them, and re-layouts  1.87 us (2%)
    ppermute x1, waiting for transfers between devices, branch(): moved = lax.ppermute(block, 'context', route) if distance else block  21.2 us
    all_to_all x1, blocking collectives, body(): all_values = lax.all_to_all(values, 'context', 0, 0)  12.1 us
    all_to_all x1, starting transfers between devices, branch(): return (moved, lax.all_to_all(attend(*operands), 'context', 0, 0))  12 us
    all_gather x1, waiting for transfers between devices, body(): received = lax.all_gather(moved, 'tensor')  12 us
    ppermute x1, starting transfers between devices, branch(): moved = lax.ppermute(block, 'context', route) if distance else block  8.03 us
    all_to_all x1, waiting for transfers between devices, body(): terms = lax.all_to_all(columns, 'tensor', 0, 0)  6.2 us
    pallas_call x1, Pallas kernels, attend(): pl.pallas_call(attention_kernel, out_shape=jax.ShapeDtypeStruct((MEMBERS,...  4.93 us
    all_to_all x1, starting transfers between devices, body(): terms = lax.all_to_all(columns, 'tensor', 0, 0)  3.24 us
  transfers between devices with their start and end apart: 4, of which 3 were waited for; matrix products, arithmetic and copies ran while one was open for 1% of the time, Pallas kernels for 5%

profile of v2, /device:TPU:1, one launch (start us, length us, event | category | flops | bytes accessed | tf_op | source)
XLA Modules:
  0.0 107.9 jit_solution(2265453148407731597)
XLA Ops:
  7.2 0.0 copy-start
  7.2 0.0 all-gather.3.cloned.1.call-start
  7.2 0.6 copy-done
  7.9 0.5 constant_dynamic-slice_fusion
  10.3 1.3 %update.1 = bf16[576,256]{1,0:T(8,128)(2,1)S(1)} custom-call(s32[4]{0:T(128)} %lengths.1, bf16[4,2,576]{2,1,0:T(2,128)(2,1)} %entries.1, bf16[4,576,256]{2,1,0:T(8,128)(2,1)} %bitcast.33), custom_call_target="tpu_custom_call" | custom-call | tf_op jit(solution)/shard_map/update/pallas_call | solution.py:162
  11.6 46.4 %conditional.1 = (bf16[576,256]{1,0:T(8,128)(2,1)S(1)}, bf16[16,80,128]{2,1,0:T(8,128)(2,1)}) conditional(s32[]{:T(128)} %clamp.3, (s32[4]{0:T(128)}, bf16[4,2,576]{2,1,0:T(2,128)(2,1)}, bf16[4,32,576]{2,1,0:T(8,128)(2,1)}, bf16[4,576,256]{2,1,0:T(8,128)(2,1)}, bf16[4,576,256]{2,1,0:T(8,128)(2,1)}, ...), branch_computations={%region_0.1_spmd, %region_1.2_spmd, %region_2.3_spmd, %region_3.4_... | conditional | flops 300000000 | bytes 6752600 | solution.py:176
  11.8 4.9 %attend.28 = bf16[16,80,128]{2,1,0:T(8,128)(2,1)} custom-call(s32[4]{0:T(128)} %get-tuple-element.309.lengths, bf16[4,2,576]{2,1,0:T(2,128)(2,1)} %get-tuple-element.310.entries, bf16[4,32,576]{2,1,0:T(8,128)(2,1)} %get-tuple-element.311.queries, bf16[4,576,256]{2,1,0:T(8,128)(2,1)} %get-tuple-element.312.staying, ...), custom_call_target="tpu_custom_call" | custom-call | flops 300000000 | bytes 4000000 | tf_op jit(solution)/shard_map/cond/branch_12_fun/attend/pallas_call | solution.py:134
  16.8 12.0 %all-to-all-start.12 = ((bf16[16,80,128]{2,1,0:T(8,128)(2,1)}), bf16[16,80,128]{2,1,0:T(8,128)(2,1)}, u32[]{:S(2)}, u32[]{:S(2)}) async-start(bf16[16,80,128]{2,1,0:T(8,128)(2,1)} %attend.28), calls=%async_computation.12 | async-start | bytes 655360 | tf_op jit(solution)/shard_map/cond/branch_12_fun/all_to_all | solution.py:151
  28.8 8.0 %collective-permute-start.11 = (bf16[576,256]{1,0:T(8,128)(2,1)S(1)}, bf16[576,256]{1,0:T(8,128)(2,1)S(1)}, u32[]{:S(2)}, u32[]{:S(2)}) collective-permute-start(bf16[576,256]{1,0:T(8,128)(2,1)S(1)} %get-tuple-element.308), channel_id=1, source_target_pairs={{16,0},{20,4},{24,8},{28,12},{32,16},{36,20},{40,24},{44,28},{48,3... | collective-permute-start | bytes 884744 | tf_op jit(solution)/shard_map/cond/branch_12_fun/ppermute | solution.py:150
  36.8 21.2 %collective-permute-done.11 = bf16[576,256]{1,0:T(8,128)(2,1)S(1)} collective-permute-done((bf16[576,256]{1,0:T(8,128)(2,1)S(1)}, bf16[576,256]{1,0:T(8,128)(2,1)S(1)}, u32[]{:S(2)}, u32[]{:S(2)}) %collective-permute-start.11) | collective-permute-done | bytes 294944 | tf_op jit(solution)/shard_map/cond/branch_12_fun/ppermute | solution.py:150
  58.0 0.0 all-to-all-done.12
  58.1 0.0 copy-start.2
  58.1 0.0 copy-start.1
  58.1 0.7 copy-done.2
  58.8 0.0 all-gather.3.cloned.1.call-update
  58.8 2.0 %merge.1 = bf16[16,8,128]{2,1,0:T(8,128)(2,1)} custom-call(bf16[16,80,128]{2,1,0:T(8,128)(2,1)} %get-tuple-element.340.arrived), custom_call_target="tpu_custom_call" | custom-call | tf_op jit(solution)/shard_map/merge/pallas_call | solution.py:183
  60.8 12.1 %all_to_all.75.values = bf16[16,8,128]{2,1,0:T(8,128)(2,1)} all-to-all(bf16[16,8,128]{2,1,0:T(8,128)(2,1)} %merge.1), channel_id=1, replica_groups=mesh['dp'=8,'context'=16,'tensor'=4] {'context'}, dimensions={0} | all-to-all | bytes 65536 | tf_op jit(solution)/shard_map/all_to_all | solution.py:190
  72.9 2.8 %project.1.columns = f32[4,8,112]{2,1,0:T(8,128)} custom-call(bf16[16,8,128]{2,1,0:T(8,128)(2,1)} %all_to_all.75.values, bf16[448,2048]{1,0:T(8,128)(2,1)} %bitcast.67), custom_call_target="tpu_custom_call" | custom-call | tf_op jit(solution)/shard_map/project/pallas_call | solution.py:192
  75.7 3.2 %all-to-all-start.17 = ((f32[4,8,112]{2,1,0:T(8,128)}), f32[4,8,112]{2,1,0:T(8,128)S(1)}, u32[]{:S(2)}, u32[]{:S(2)}) async-start(f32[4,8,112]{2,1,0:T(8,128)} %project.1.columns), calls=%async_computation.17 | async-start | bytes 32768 | tf_op jit(solution)/shard_map/all_to_all | solution.py:199
  79.0 1.0 keep.1.cache_in
  80.0 6.2 %all-to-all-done.17 = f32[4,8,112]{2,1,0:T(8,128)S(1)} async-done(((f32[4,8,112]{2,1,0:T(8,128)}), f32[4,8,112]{2,1,0:T(8,128)S(1)}, u32[]{:S(2)}, u32[]{:S(2)}) %all-to-all-start.17) | async-done | bytes 14368 | tf_op jit(solution)/shard_map/all_to_all | solution.py:199
  86.2 0.6 reduce_sum.9
  86.8 12.0 %all-gather.3.cloned.1.call-done = bf16[2304,256]{1,0:T(8,128)(2,1)} async-done(((bf16[576,256]{1,0:T(8,128)(2,1)}), bf16[2304,256]{1,0:T(8,128)(2,1)}) %all-gather.3.cloned.1.call-update) | async-done | bytes 1179664 | tf_op jit(solution)/shard_map/all_gather | solution.py:181
  98.8 2.3 %fill.1 = bf16[4,576,512]{2,1,0:T(8,128)(2,1)} custom-call(bf16[4,576,512]{2,1,0:T(8,128)(2,1)} %keep.1.cache_in, bf16[4,576,256]{2,1,0:T(8,128)(2,1)} %bitcast.68), custom_call_target="tpu_custom_call", output_to_operand_aliasing={{}: (0, {})} | custom-call | tf_op jit(solution)/shard_map/fill/pallas_call | solution.py:211
  (2 shorter events, 0.0 us)
Async XLA Ops:
  7.2 0.7 copy-start
  7.2 91.6 %all-gather.3.cloned.1.call-start = ((), (), s32[]{:S(2)}) async-start(), calls=%async_computation.18 | async-start | bytes 1474560 | tf_op jit(solution)/shard_map/all_gather | solution.py:181
  16.8 41.3 %all-to-all-start.12 = ((bf16[16,80,128]{2,1,0:T(8,128)(2,1)}), bf16[16,80,128]{2,1,0:T(8,128)(2,1)}, u32[]{:S(2)}, u32[]{:S(2)}) async-start(bf16[16,80,128]{2,1,0:T(8,128)(2,1)} %attend.28), calls=%async_computation.12 | async-start | bytes 655360 | tf_op jit(solution)/shard_map/cond/branch_12_fun/all_to_all | solution.py:151
  28.8 29.2 %collective-permute-start.11 = (bf16[576,256]{1,0:T(8,128)(2,1)S(1)}, bf16[576,256]{1,0:T(8,128)(2,1)S(1)}, u32[]{:S(2)}, u32[]{:S(2)}) collective-permute-start(bf16[576,256]{1,0:T(8,128)(2,1)S(1)} %get-tuple-element.308), channel_id=1, source_target_pairs={{16,0},{20,4},{24,8},{28,12},{32,16},{36,20},{40,24},{44,28},{48,3... | collective-permute-start | bytes 884744 | tf_op jit(solution)/shard_map/cond/branch_12_fun/ppermute | solution.py:150
  58.1 0.7 copy-start.2
  58.1 20.9 %copy-start.1 = (bf16[1,4,256,576]{2,3,1,0:T(8,128)(2,1)S(1)}, bf16[1,4,256,576]{2,3,1,0:T(8,128)(2,1)}, u32[]{:S(2)}) copy-start(bf16[1,4,256,576]{2,3,1,0:T(8,128)(2,1)} %param.24) | copy-start | bytes 3538948
  75.7 10.5 %all-to-all-start.17 = ((f32[4,8,112]{2,1,0:T(8,128)}), f32[4,8,112]{2,1,0:T(8,128)S(1)}, u32[]{:S(2)}, u32[]{:S(2)}) async-start(f32[4,8,112]{2,1,0:T(8,128)} %project.1.columns), calls=%async_computation.17 | async-start | bytes 32768 | tf_op jit(solution)/shard_map/all_to_all | solution.py:199
Sparse Core Ops, SparseCore 0:
  58.9 39.7 all-gather.2

commit v3 on v2

v3 whole, which is shorter than its diff:
```python
import jax
import jax.numpy as jnp
from jax import lax
from jax.experimental import pallas as pl
from jax.experimental.pallas import tpu as pltpu
from jax.sharding import PartitionSpec as P

REQ = 4
STEPS = 2
HEADS = 16
LATENT = 512
WIDTH = 576
SLICE = 256
MEMBERS = 16
TENSOR = 4
LANES = 128
CHUNK = WIDTH * SLICE // (MEMBERS * LANES)
ROWS = REQ * STEPS
LTILES = LATENT // LANES
VROWS = LATENT // MEMBERS
STATS = LTILES * ROWS
VALUE = STATS + ROWS
CACHE = VALUE + VROWS
OUTC = 112
PART = 2 * ROWS
PIECES = 2
PIECE = WIDTH // PIECES
FORTH_0 = 0
FORTH_FAR = WIDTH
FORTH_NEAR = FORTH_FAR + PART
FORTH_1 = FORTH_NEAR + PART
FORTH_ROWS = FORTH_1 + WIDTH
BACK_0 = PART
BACK_1 = BACK_0 + WIDTH
BACK_ROWS = BACK_1 + WIDTH

softmax_scale = 0.07216878364870322
large_negative = -1e30

f32 = jnp.float32
bf16 = jnp.bfloat16

VMEM = pl.BlockSpec(memory_space=pltpu.VMEM)
SMEM = pl.BlockSpec(memory_space=pltpu.SMEM)
ANY = pl.BlockSpec(memory_space=pl.ANY)


def nt_dot(a, b):
    return lax.dot_general(a, b, (((1,), (1,)), ((), ())), preferred_element_type=f32)


def attend_kernel(
    lengths, entries, queries, staying_hbm, leaving_hbm, w_value, out, staying, leaving, sems
):
    member = lax.axis_index("context")
    tensor = lax.axis_index("tensor")
    copies = []
    for b in range(REQ):
        copies.append(
            (
                pltpu.make_async_copy(staying_hbm.at[b], staying.at[b], sems.at[0, b]),
                pltpu.make_async_copy(leaving_hbm.at[b], leaving.at[b], sems.at[1, b]),
            )
        )
    for pair in copies:
        for copy in pair:
            copy.start()
    out[:, VALUE : VALUE + VROWS, :] = w_value[...]
    first_kept = member * SLICE
    first_moved = (MEMBERS + member) * SLICE
    row = lax.broadcasted_iota(jnp.int32, (STEPS * HEADS, SLICE), 0)
    slot = lax.broadcasted_iota(jnp.int32, (STEPS * HEADS, SLICE), 1)
    step = (row >= HEADS).astype(jnp.int32)
    lane = lax.broadcasted_iota(jnp.int32, (STEPS * HEADS, LANES), 1)
    parts = []
    for b in range(REQ):
        for copy in copies[b]:
            copy.wait()
        new_slot = lengths[b] - first_moved

        @pl.when((new_slot + STEPS > 0) & (new_slot < SLICE))
        def _():
            slots = lax.broadcasted_iota(jnp.int32, (STEPS, SLICE), 1)
            steps = lax.broadcasted_iota(jnp.int32, (STEPS, SLICE), 0)
            hit = (slots == new_slot + steps).astype(f32)
            placed = lax.dot_general(
                entries[b], hit.astype(bf16), (((0,), (0,)), ((), ())), preferred_element_type=f32
            )
            taken = jnp.max(hit, axis=0, keepdims=True) > 0.5
            leaving[b] = jnp.where(taken, placed, leaving[b].astype(f32)).astype(bf16)

        q = queries[b]
        limit = lengths[b] + 1 + step
        use_kept = slot + first_kept < limit
        use_moved = slot + first_moved < limit
        kept_scores = jnp.dot(q, staying[b], preferred_element_type=f32) * softmax_scale
        moved_scores = jnp.dot(q, leaving[b], preferred_element_type=f32) * softmax_scale
        kept_scores = jnp.where(use_kept, kept_scores, large_negative)
        moved_scores = jnp.where(use_moved, moved_scores, large_negative)
        peak = jnp.maximum(
            jnp.max(kept_scores, axis=1, keepdims=True),
            jnp.max(moved_scores, axis=1, keepdims=True),
        )
        peak = peak.astype(bf16).astype(f32)
        kept_w = jnp.where(use_kept, jnp.exp(kept_scores - peak), 0.0).astype(bf16)
        moved_w = jnp.where(use_moved, jnp.exp(moved_scores - peak), 0.0).astype(bf16)
        numerator = nt_dot(kept_w, staying[b, 0:LATENT, :]) + nt_dot(
            moved_w, leaving[b, 0:LATENT, :]
        )
        total = jnp.sum(kept_w.astype(f32) + moved_w.astype(f32), axis=1, keepdims=True)
        high = total.astype(bf16).astype(f32)
        stats = jnp.where(
            lane == 0, peak, jnp.where(lane == 1, high, jnp.where(lane == 2, total - high, 0.0))
        )
        both = jnp.concatenate([numerator, stats], axis=1)
        parts += [both[:HEADS], both[HEADS:]]
    by_head = jnp.transpose(jnp.stack(parts), (1, 0, 2))
    tiles = [by_head[:, :, i * LANES : (i + 1) * LANES] for i in range(LTILES + 1)]
    out[:, 0:VALUE, :] = jnp.concatenate(tiles, axis=1).astype(bf16)
    block = leaving[tensor]
    for c in range(MEMBERS):
        at, lanes = (c % 8) * CHUNK, (c // 8) * LANES
        out[c, CACHE : CACHE + CHUNK, :] = block[at : at + CHUNK, lanes : lanes + LANES]


def merge_kernel(pairing, arrived, out):
    offset = pairing[lax.axis_index("tensor"), 0]
    rows = arrived[:, 0:VALUE, :].astype(f32)
    stats = rows[:, STATS:VALUE, :]
    peak = stats[:, :, 0:1]
    top = jnp.max(peak, axis=0, keepdims=True)
    factor = jnp.exp(peak - top)
    total = jnp.sum(factor * (stats[:, :, 1:2] + stats[:, :, 2:3]), axis=0)
    weights = arrived[:, VALUE : VALUE + VROWS, :].reshape(LATENT, LANES)
    values = jnp.zeros((ROWS, LANES), f32)
    for i in range(LTILES):
        numerator = jnp.sum(factor * rows[:, ROWS * i : ROWS * (i + 1), :], axis=0)
        latent = (numerator / total).astype(bf16)
        values += jnp.dot(
            latent, weights[i * LANES : (i + 1) * LANES], preferred_element_type=f32
        )
    values = values.astype(bf16)
    for r in range(MEMBERS):
        source = lax.rem(r + MEMBERS - offset, MEMBERS)
        out[r, 0:CHUNK, :] = arrived[source, CACHE : CACHE + CHUNK, :]
        out[r, CHUNK : CHUNK + ROWS, :] = values


def project_kernel(handed, w_out, forth, back, mine):
    tensor = lax.axis_index("tensor")
    for c in range(MEMBERS):
        at = CHUNK * (c % 8)
        forth[(FORTH_0, FORTH_1)[c // 8] + at : (FORTH_0, FORTH_1)[c // 8] + at + CHUNK, :] = (
            handed[c, 0:CHUNK, :]
        )
        back[(BACK_0, BACK_1)[c // 8] + at : (BACK_0, BACK_1)[c // 8] + at + CHUNK, :] = (
            handed[c, 0:CHUNK, :]
        )
    flat = jnp.concatenate([handed[h, CHUNK : CHUNK + ROWS, :] for h in range(HEADS)], axis=1)
    columns = nt_dot(flat, w_out[...])
    pad = jnp.zeros((ROWS, LANES - OUTC), f32)
    parts = [
        jnp.concatenate([columns[:, OUTC * t : OUTC * (t + 1)], pad], axis=1)
        for t in range(TENSOR)
    ]

    def part_of(distance):
        target = lax.rem(tensor + distance, TENSOR)
        part = parts[0]
        for t in range(1, TENSOR):
            part = jnp.where(target == t, parts[t], part)
        return part

    def pieces(part):
        high = part.astype(bf16)
        return jnp.concatenate([high, (part - high.astype(f32)).astype(bf16)], axis=0)

    mine[...] = part_of(0)
    forth[FORTH_NEAR : FORTH_NEAR + PART, :] = pieces(part_of(1))
    forth[FORTH_FAR : FORTH_FAR + PART, :] = pieces(part_of(2))
    back[0:PART, :] = pieces(part_of(3))


def stores(block, first, cache, request, half, sems):
    lanes = SLICE + half * LANES
    return [
        pltpu.make_async_copy(
            block.at[first + PIECE * i : first + PIECE * (i + 1), :],
            cache.at[request, PIECE * i : PIECE * (i + 1), lanes : lanes + LANES],
            sems.at[i],
        )
        for i in range(PIECES)
    ]


def finish_all(copies):
    for copy in copies:
        copy.start()
    for copy in copies:
        copy.wait()


def keep_kernel(staying, forth, cache, sem, sems):
    tensor = lax.axis_index("tensor")
    finish_all(
        [pltpu.make_async_copy(staying, cache.at[:, :, 0:SLICE], sem)]
        + stores(forth, FORTH_0, cache, tensor, 0, sems.at[0])
        + stores(forth, FORTH_1, cache, tensor, 1, sems.at[1])
    )


def joined(pieces):
    pieces = pieces.astype(f32)
    return pieces[:ROWS] + pieces[ROWS:]


def near_kernel(cache_in, from_left, from_right, mine, cache, total, sems):
    tensor = lax.axis_index("tensor")
    left = lax.rem(tensor + TENSOR - 1, TENSOR)
    right = lax.rem(tensor + 1, TENSOR)
    total[...] = (
        mine[...]
        + joined(from_left[FORTH_NEAR : FORTH_NEAR + PART, :])
        + joined(from_right[0:PART, :])
    )
    finish_all(
        stores(from_left, FORTH_0, cache, left, 0, sems.at[0])
        + stores(from_left, FORTH_1, cache, left, 1, sems.at[1])
        + stores(from_right, BACK_0, cache, right, 0, sems.at[2])
        + stores(from_right, BACK_1, cache, right, 1, sems.at[3])
    )


def far_kernel(cache_in, far_left, far_right, near_total, cache, attn, sems):
    across = lax.rem(lax.axis_index("tensor") + 2, TENSOR)
    copies = stores(far_left, 0, cache, across, 0, sems.at[0])
    copies += stores(far_right, 0, cache, across, 1, sems.at[1])
    for copy in copies:
        copy.start()
    total = near_total[...] + joined(far_left[FORTH_FAR : FORTH_FAR + PART, :])
    attn[...] = total[:, :OUTC].astype(bf16)
    for copy in copies:
        copy.wait()


def body(staying_cache, leaving_cache, lengths, pairing, new_entries, queries, w_value, w_out):
    staying = jnp.swapaxes(staying_cache[0], 1, 2)
    leaving = jnp.swapaxes(leaving_cache[0], 1, 2)
    q = queries.reshape(REQ, STEPS * HEADS, WIDTH)

    first = pl.pallas_call(
        attend_kernel,
        out_shape=jax.ShapeDtypeStruct((MEMBERS, CACHE + CHUNK, LANES), bf16),
        in_specs=[SMEM, VMEM, VMEM, ANY, ANY, VMEM],
        out_specs=VMEM,
        scratch_shapes=[
            pltpu.VMEM((REQ, WIDTH, SLICE), bf16),
            pltpu.VMEM((REQ, WIDTH, SLICE), bf16),
            pltpu.SemaphoreType.DMA((2, REQ)),
        ],
        name="attend",
    )(lengths, new_entries, q, staying, leaving, w_value)
    arrived = lax.all_to_all(first, "context", 0, 0)

    second = pl.pallas_call(
        merge_kernel,
        out_shape=jax.ShapeDtypeStruct((MEMBERS, CHUNK + ROWS, LANES), bf16),
        in_specs=[SMEM, VMEM],
        out_specs=VMEM,
        name="merge",
    )(pairing, arrived)
    handed = lax.all_to_all(second, "context", 0, 0)

    forth, back, mine = pl.pallas_call(
        project_kernel,
        out_shape=(
            jax.ShapeDtypeStruct((FORTH_ROWS, LANES), bf16),
            jax.ShapeDtypeStruct((BACK_ROWS, LANES), bf16),
            jax.ShapeDtypeStruct((ROWS, LANES), f32),
        ),
        in_specs=[VMEM, VMEM],
        out_specs=(VMEM, VMEM, VMEM),
        name="project",
    )(handed, w_out.T)

    up = [((t - 1) % TENSOR, t) for t in range(TENSOR)]
    down = [((t + 1) % TENSOR, t) for t in range(TENSOR)]
    from_left = lax.ppermute(forth, "tensor", up)
    from_right = lax.ppermute(back, "tensor", down)
    far_left = lax.ppermute(from_left[0 : FORTH_FAR + PART], "tensor", up)
    far_right = lax.ppermute(from_right[BACK_1:], "tensor", down)

    whole = jax.ShapeDtypeStruct((REQ, WIDTH, 2 * SLICE), bf16)
    cache = pl.pallas_call(
        keep_kernel,
        out_shape=whole,
        in_specs=[VMEM, VMEM],
        out_specs=ANY,
        scratch_shapes=[pltpu.SemaphoreType.DMA, pltpu.SemaphoreType.DMA((2, PIECES))],
        cost_estimate=pl.CostEstimate(flops=0, bytes_accessed=8_000_000, transcendentals=0),
        name="keep",
    )(staying, forth)
    cache, near_total = pl.pallas_call(
        near_kernel,
        out_shape=(whole, jax.ShapeDtypeStruct((ROWS, LANES), f32)),
        in_specs=[ANY, VMEM, VMEM, VMEM],
        out_specs=(ANY, VMEM),
        scratch_shapes=[pltpu.SemaphoreType.DMA((4, PIECES))],
        input_output_aliases={0: 0},
        cost_estimate=pl.CostEstimate(flops=0, bytes_accessed=4_000_000, transcendentals=0),
        name="near",
    )(cache, from_left, from_right, mine)
    cache, attn_out = pl.pallas_call(
        far_kernel,
        out_shape=(whole, jax.ShapeDtypeStruct((ROWS, OUTC), bf16)),
        in_specs=[ANY, VMEM, VMEM, VMEM],
        out_specs=(ANY, VMEM),
        scratch_shapes=[pltpu.SemaphoreType.DMA((2, PIECES))],
        input_output_aliases={0: 0},
        name="far",
    )(cache, far_left, far_right, near_total)
    attn_out = attn_out.reshape(REQ, STEPS, OUTC)
    return (jnp.swapaxes(cache, 1, 2)[None], attn_out)


def solution(mesh):
    placed = (
        P("context", "dp", None, None),
        P("context", "dp", None, None),
        P("dp"),
        P("dp", None),
        P("dp", None, None),
        P("dp", None, "tensor", None),
        P("tensor", "context", None),
        P("tensor", "context"),
    )
    return jax.shard_map(
        body,
        mesh=mesh,
        in_specs=placed,
        out_specs=(P("context", "dp", None, None), P("dp", None, ("context", "tensor"))),
        check_vma=False,
    )
```

time: 108 us -> 92.7 us (0.86)
  the two profiles are of different devices: /device:TPU:1 before, /device:TPU:146 now
where the time goes in v3:
time: 92.7 us; the launch traced here: 92.1 us
  blocking collectives  43.4 us (47%)
  Pallas kernels  17.6 us (19%)
  starting transfers between devices  15.2 us (16%)
  waiting for transfers between devices  14.4 us (16%)
    all_to_all x1, blocking collectives, body(): arrived = lax.all_to_all(first, 'context', 0, 0)  27 us
    all_to_all x1, blocking collectives, body(): handed = lax.all_to_all(second, 'context', 0, 0)  16.4 us
    ppermute x1, waiting for transfers between devices, body(): from_left = lax.ppermute(forth, 'tensor', up)  10.1 us
    ppermute x1, starting transfers between devices, body(): far_left = lax.ppermute(from_left[0:FORTH_FAR + PART], 'tensor', up)  6.59 us
    pallas_call x1, Pallas kernels, body(): pl.pallas_call(attend_kernel, out_shape=jax.ShapeDtypeStruct((MEMBERS, CA...  5 us
    ppermute x1, starting transfers between devices, body(): from_left = lax.ppermute(forth, 'tensor', up)  4.8 us
    ppermute x1, waiting for transfers between devices, body(): far_right = lax.ppermute(from_right[BACK_1:], 'tensor', down)  4.3 us
    pallas_call x1, Pallas kernels, body(): pl.pallas_call(project_kernel, out_shape=(jax.ShapeDtypeStruct((FORTH_ROW...  3.1 us
  transfers between devices with their start and end apart: 4, of which 2 were waited for; matrix products, arithmetic and copies ran while one was open for 0% of the time, Pallas kernels for 5%

profile of v3, /device:TPU:146, one launch (start us, length us, event | category | flops | bytes accessed | tf_op | source)
XLA Modules:
  0.0 92.1 jit_solution(17428726429332302003)
XLA Ops:
  0.6 5.0 %attend.1 = bf16[16,144,128]{2,1,0:T(8,128)(2,1)} custom-call(s32[4]{0:T(128)} %lengths.1, bf16[4,2,576]{2,1,0:T(2,128)(2,1)} %entries.1, bf16[4,32,576]{2,1,0:T(8,128)(2,1)} %bitcast.17, bf16[4,576,256]{2,1,0:T(8,128)(2,1)} %bitcast.13, bf16[4,576,256]{2,1,0:T(8,128)(2,1)} %bitcast.16, bf16[16,32,128]{2,1,0:T(8,128)(2,1)} %w_value.1), custom_call_target="tpu_custom_call" | custom-call | tf_op jit(solution)/shard_map/attend/pallas_call | solution.py:251
  5.6 27.0 %all_to_all.10.arrived = bf16[16,144,128]{2,1,0:T(8,128)(2,1)} all-to-all(bf16[16,144,128]{2,1,0:T(8,128)(2,1)} %attend.1), channel_id=1, replica_groups=mesh['dp'=8,'context'=16,'tensor'=4] {'context'}, dimensions={0} | all-to-all | bytes 1179648 | tf_op jit(solution)/shard_map/all_to_all | solution.py:263
  32.6 2.2 %merge.1 = bf16[16,80,128]{2,1,0:T(8,128)(2,1)} custom-call(s32[4,16]{1,0:T(4,128)} %pairing.1, bf16[16,144,128]{2,1,0:T(8,128)(2,1)} %all_to_all.10.arrived), custom_call_target="tpu_custom_call" | custom-call | tf_op jit(solution)/shard_map/merge/pallas_call | solution.py:265
  34.8 16.4 %all_to_all.11.handed = bf16[16,80,128]{2,1,0:T(8,128)(2,1)} all-to-all(bf16[16,80,128]{2,1,0:T(8,128)(2,1)} %merge.1), channel_id=1, replica_groups=mesh['dp'=8,'context'=16,'tensor'=4] {'context'}, dimensions={0} | all-to-all | bytes 655360 | tf_op jit(solution)/shard_map/all_to_all | solution.py:272
  51.2 3.1 %project.1 = (bf16[1184,128]{1,0:T(8,128)(2,1)}, bf16[1168,128]{1,0:T(8,128)(2,1)}, f32[8,128]{1,0:T(8,128)}) custom-call(bf16[16,80,128]{2,1,0:T(8,128)(2,1)} %all_to_all.11.handed, bf16[448,2048]{1,0:T(8,128)(2,1)} %bitcast.15), custom_call_target="tpu_custom_call" | custom-call | tf_op jit(solution)/shard_map/project/pallas_call | solution.py:274
  54.3 4.8 %collective-permute-start = (bf16[1184,128]{1,0:T(8,128)(2,1)}, bf16[1184,128]{1,0:T(8,128)(2,1)S(1)}, u32[]{:S(2)}, u32[]{:S(2)}) collective-permute-start(bf16[1184,128]{1,0:T(8,128)(2,1)} %get-tuple-element.9.forth), channel_id=1, source_target_pairs={{3,0},{0,1},{1,2},{2,3},{7,4},{4,5},{5,6},{6,7},{11,8},{8,9},{9,10... | collective-permute-start | bytes 909320 | tf_op jit(solution)/shard_map/ppermute | solution.py:288
  59.1 1.9 %collective-permute-start.1 = (bf16[1168,128]{1,0:T(8,128)(2,1)}, bf16[1168,128]{1,0:T(8,128)(2,1)S(1)}, u32[]{:S(2)}, u32[]{:S(2)}) collective-permute-start(bf16[1168,128]{1,0:T(8,128)(2,1)} %get-tuple-element.10), channel_id=1, source_target_pairs={{1,0},{2,1},{3,2},{0,3},{5,4},{6,5},{7,6},{4,7},{9,8},{10,9},{11,1... | collective-permute-start | bytes 897032 | tf_op jit(solution)/shard_map/ppermute | solution.py:289
  61.1 10.1 %collective-permute-done.from_left = bf16[1184,128]{1,0:T(8,128)(2,1)S(1)} collective-permute-done((bf16[1184,128]{1,0:T(8,128)(2,1)}, bf16[1184,128]{1,0:T(8,128)(2,1)S(1)}, u32[]{:S(2)}, u32[]{:S(2)}) %collective-permute-start) | collective-permute-done | bytes 303136 | tf_op jit(solution)/shard_map/ppermute | solution.py:288
  71.2 0.0 copy-start
  71.2 6.6 %collective-permute-start.2 = (bf16[592,128]{1,0:T(8,128)(2,1)S(1)}, bf16[592,128]{1,0:T(8,128)(2,1)S(1)}, u32[]{:S(2)}, u32[]{:S(2)}) collective-permute-start(bf16[592,128]{1,0:T(8,128)(2,1)S(1)} %slice.8), channel_id=1, source_target_pairs={{3,0},{0,1},{1,2},{2,3},{7,4},{4,5},{5,6},{6,7},{11,8},{8,9},{9,10... | collective-permute-start | bytes 454664 | tf_op jit(solution)/shard_map/ppermute | solution.py:290
  77.8 0.0 collective-permute-done.1.from_right
  77.8 0.0 copy-start.1
  77.8 1.9 %collective-permute-start.3 = (bf16[576,128]{1,0:T(8,128)(2,1)S(1)}, bf16[576,128]{1,0:T(8,128)(2,1)S(1)}, u32[]{:S(2)}, u32[]{:S(2)}) collective-permute-start(bf16[576,128]{1,0:T(8,128)(2,1)S(1)} %slice.9), channel_id=1, source_target_pairs={{1,0},{2,1},{3,2},{0,3},{5,4},{6,5},{7,6},{4,7},{9,8},{10,9},{11,1... | collective-permute-start | bytes 442376 | tf_op jit(solution)/shard_map/ppermute | solution.py:291
  79.8 2.5 %keep.1.cache_in = bf16[4,576,512]{2,1,0:T(8,128)(2,1)} custom-call(bf16[4,576,256]{2,1,0:T(8,128)(2,1)} %bitcast.14, bf16[1184,128]{1,0:T(8,128)(2,1)} %get-tuple-element.9.forth), custom_call_target="tpu_custom_call" | custom-call | bytes 8000000 | tf_op jit(solution)/shard_map/keep/pallas_call | solution.py:294
  82.2 0.0 copy-done
  82.2 0.0 copy-done.1
  82.2 2.5 %near.1 = (bf16[4,576,512]{2,1,0:T(8,128)(2,1)}, f32[8,128]{1,0:T(8,128)}) custom-call(bf16[4,576,512]{2,1,0:T(8,128)(2,1)} %keep.1.cache_in, bf16[1184,128]{1,0:T(8,128)(2,1)} %copy-done, bf16[1168,128]{1,0:T(8,128)(2,1)} %copy-done.1, f32[8,128]{1,0:T(8,128)} %get-tuple-element.11.mine), custom_call_target="tpu_custom_call", output_to_operand_aliasing={{0}: (0, {})} | custom-call | bytes 4000000 | tf_op jit(solution)/shard_map/near/pallas_call | solution.py:303
  84.8 4.3 %collective-permute-done.3.far_right = bf16[576,128]{1,0:T(8,128)(2,1)S(1)} collective-permute-done((bf16[576,128]{1,0:T(8,128)(2,1)S(1)}, bf16[576,128]{1,0:T(8,128)(2,1)S(1)}, u32[]{:S(2)}, u32[]{:S(2)}) %collective-permute-start.3) | collective-permute-done | bytes 147488 | tf_op jit(solution)/shard_map/ppermute | solution.py:291
  89.1 0.0 copy-start.3
  89.1 0.0 collective-permute-done.2.far_left
  89.1 0.0 copy-start.2
  89.1 0.7 copy-done.3
  89.7 0.1 copy-done.2
  89.8 2.3 %far.1 = (bf16[4,576,512]{2,1,0:T(8,128)(2,1)}, bf16[8,112]{1,0:T(8,128)(2,1)}) custom-call(bf16[4,576,512]{2,1,0:T(8,128)(2,1)} %get-tuple-element.12.cache_in, bf16[592,128]{1,0:T(8,128)(2,1)} %copy-done.2, bf16[576,128]{1,0:T(8,128)(2,1)} %copy-done.3, f32[8,128]{1,0:T(8,128)} %get-tuple-element.13.near_total), custom_call_target="tpu_custom_call", output_to_operand_aliasing={{0}: (0, {})} | custom-call | tf_op jit(solution)/shard_map/far/pallas_call | solution.py:313
  (2 shorter events, 0.0 us)
Async XLA Ops:
  54.3 16.9 %collective-permute-start = (bf16[1184,128]{1,0:T(8,128)(2,1)}, bf16[1184,128]{1,0:T(8,128)(2,1)S(1)}, u32[]{:S(2)}, u32[]{:S(2)}) collective-permute-start(bf16[1184,128]{1,0:T(8,128)(2,1)} %get-tuple-element.9.forth), channel_id=1, source_target_pairs={{3,0},{0,1},{1,2},{2,3},{7,4},{4,5},{5,6},{6,7},{11,8},{8,9},{9,10... | collective-permute-start | bytes 909320 | tf_op jit(solution)/shard_map/ppermute | solution.py:288
  59.1 18.7 %collective-permute-start.1 = (bf16[1168,128]{1,0:T(8,128)(2,1)}, bf16[1168,128]{1,0:T(8,128)(2,1)S(1)}, u32[]{:S(2)}, u32[]{:S(2)}) collective-permute-start(bf16[1168,128]{1,0:T(8,128)(2,1)} %get-tuple-element.10), channel_id=1, source_target_pairs={{1,0},{2,1},{3,2},{0,3},{5,4},{6,5},{7,6},{4,7},{9,8},{10,9},{11,1... | collective-permute-start | bytes 897032 | tf_op jit(solution)/shard_map/ppermute | solution.py:289
  71.2 11.0 %copy-start = (bf16[1184,128]{1,0:T(8,128)(2,1)}, bf16[1184,128]{1,0:T(8,128)(2,1)S(1)}, u32[]{:S(2)}) copy-start(bf16[1184,128]{1,0:T(8,128)(2,1)S(1)} %collective-permute-done.from_left) | copy-start | bytes 909316
  71.2 17.9 %collective-permute-start.2 = (bf16[592,128]{1,0:T(8,128)(2,1)S(1)}, bf16[592,128]{1,0:T(8,128)(2,1)S(1)}, u32[]{:S(2)}, u32[]{:S(2)}) collective-permute-start(bf16[592,128]{1,0:T(8,128)(2,1)S(1)} %slice.8), channel_id=1, source_target_pairs={{3,0},{0,1},{1,2},{2,3},{7,4},{4,5},{5,6},{6,7},{11,8},{8,9},{9,10... | collective-permute-start | bytes 454664 | tf_op jit(solution)/shard_map/ppermute | solution.py:290
  77.8 4.4 %copy-start.1 = (bf16[1168,128]{1,0:T(8,128)(2,1)}, bf16[1168,128]{1,0:T(8,128)(2,1)S(1)}, u32[]{:S(2)}) copy-start(bf16[1168,128]{1,0:T(8,128)(2,1)S(1)} %collective-permute-done.1.from_right) | copy-start | bytes 897028
  77.8 11.2 %collective-permute-start.3 = (bf16[576,128]{1,0:T(8,128)(2,1)S(1)}, bf16[576,128]{1,0:T(8,128)(2,1)S(1)}, u32[]{:S(2)}, u32[]{:S(2)}) collective-permute-start(bf16[576,128]{1,0:T(8,128)(2,1)S(1)} %slice.9), channel_id=1, source_target_pairs={{1,0},{2,1},{3,2},{0,3},{5,4},{6,5},{7,6},{4,7},{9,8},{10,9},{11,1... | collective-permute-start | bytes 442376 | tf_op jit(solution)/shard_map/ppermute | solution.py:291
  89.1 0.7 copy-start.3
  89.1 0.7 copy-start.2

commit v4 on v3

--- a/solution.py
+++ b/solution.py
@@ -19,8 +19,10 @@
 LTILES = LATENT // LANES
 VROWS = LATENT // MEMBERS
 STATS = LTILES * ROWS
-VALUE = STATS + ROWS
-CACHE = VALUE + VROWS
+CACHE = VROWS
+PARTIAL = CACHE + CHUNK
+SENT = PARTIAL + STATS + ROWS
+EARLY = 96
 OUTC = 112
 PART = 2 * ROWS
 PIECES = 2
@@ -45,27 +47,46 @@
 ANY = pl.BlockSpec(memory_space=pl.ANY)
 
 
+def grant(mib):
+    return pltpu.CompilerParams(vmem_limit_bytes=mib * 2**20)
+
+
 def nt_dot(a, b):
     return lax.dot_general(a, b, (((1,), (1,)), ((), ())), preferred_element_type=f32)
 
 
 def attend_kernel(
-    lengths, entries, queries, staying_hbm, leaving_hbm, w_value, out, staying, leaving, sems
+    lengths,
+    entries,
+    queries_hbm,
+    staying_hbm,
+    leaving_hbm,
+    w_value_hbm,
+    out_hbm,
+    queries,
+    staying,
+    leaving,
+    w_value,
+    out,
+    sems,
 ):
     member = lax.axis_index("context")
     tensor = lax.axis_index("tensor")
-    copies = []
+    kept_copies, moved_copies = [], []
     for b in range(REQ):
-        copies.append(
-            (
-                pltpu.make_async_copy(staying_hbm.at[b], staying.at[b], sems.at[0, b]),
-                pltpu.make_async_copy(leaving_hbm.at[b], leaving.at[b], sems.at[1, b]),
-            )
-        )
-    for pair in copies:
-        for copy in pair:
-            copy.start()
-    out[:, VALUE : VALUE + VROWS, :] = w_value[...]
+        moved_copies.append(
+            pltpu.make_async_copy(leaving_hbm.at[b], leaving.at[b], sems.at[0, b])
+        )
+        moved_copies[b].start()
+    query_copy = pltpu.make_async_copy(queries_hbm, queries, sems.at[2, 0])
+    query_copy.start()
+    value_copy = pltpu.make_async_copy(w_value_hbm, w_value, sems.at[2, 1])
+    value_copy.start()
+    for b in range(REQ):
+        kept_copies.append(
+            pltpu.make_async_copy(staying_hbm.at[b], staying.at[b], sems.at[1, b])
+        )
+        kept_copies[b].start()
     first_kept = member * SLICE
     first_moved = (MEMBERS + member) * SLICE
     row = lax.broadcasted_iota(jnp.int32, (STEPS * HEADS, SLICE), 0)
@@ -74,8 +95,7 @@
     lane = lax.broadcasted_iota(jnp.int32, (STEPS * HEADS, LANES), 1)
     parts = []
     for b in range(REQ):
-        for copy in copies[b]:
-            copy.wait()
+        moved_copies[b].wait()
         new_slot = lengths[b] - first_moved
 
         @pl.when((new_slot + STEPS > 0) & (new_slot < SLICE))
@@ -89,6 +109,19 @@
             taken = jnp.max(hit, axis=0, keepdims=True) > 0.5
             leaving[b] = jnp.where(taken, placed, leaving[b].astype(f32)).astype(bf16)
 
+    block = leaving[tensor]
+    for c in range(MEMBERS):
+        at, lanes = (c % 8) * CHUNK, (c // 8) * LANES
+        out[c, CACHE : CACHE + CHUNK, :] = block[at : at + CHUNK, lanes : lanes + LANES]
+    value_copy.wait()
+    out[:, 0:VROWS, :] = w_value[...]
+    early_copy = pltpu.make_async_copy(
+        out.at[:, 0:EARLY, :], out_hbm.at[:, 0:EARLY, :], sems.at[2, 2]
+    )
+    early_copy.start()
+    query_copy.wait()
+    for b in range(REQ):
+        kept_copies[b].wait()
         q = queries[b]
         limit = lengths[b] + 1 + step
         use_kept = slot + first_kept < limit
@@ -116,22 +149,24 @@
         parts += [both[:HEADS], both[HEADS:]]
     by_head = jnp.transpose(jnp.stack(parts), (1, 0, 2))
     tiles = [by_head[:, :, i * LANES : (i + 1) * LANES] for i in range(LTILES + 1)]
-    out[:, 0:VALUE, :] = jnp.concatenate(tiles, axis=1).astype(bf16)
-    block = leaving[tensor]
-    for c in range(MEMBERS):
-        at, lanes = (c % 8) * CHUNK, (c // 8) * LANES
-        out[c, CACHE : CACHE + CHUNK, :] = block[at : at + CHUNK, lanes : lanes + LANES]
+    out[:, PARTIAL:SENT, :] = jnp.concatenate(tiles, axis=1).astype(bf16)
+    late_copy = pltpu.make_async_copy(
+        out.at[:, EARLY:SENT, :], out_hbm.at[:, EARLY:SENT, :], sems.at[2, 3]
+    )
+    late_copy.start()
+    early_copy.wait()
+    late_copy.wait()
 
 
 def merge_kernel(pairing, arrived, out):
     offset = pairing[lax.axis_index("tensor"), 0]
-    rows = arrived[:, 0:VALUE, :].astype(f32)
-    stats = rows[:, STATS:VALUE, :]
+    rows = arrived[:, PARTIAL:SENT, :].astype(f32)
+    stats = rows[:, STATS:, :]
     peak = stats[:, :, 0:1]
     top = jnp.max(peak, axis=0, keepdims=True)
     factor = jnp.exp(peak - top)
     total = jnp.sum(factor * (stats[:, :, 1:2] + stats[:, :, 2:3]), axis=0)
-    weights = arrived[:, VALUE : VALUE + VROWS, :].reshape(LATENT, LANES)
+    weights = arrived[:, 0:VROWS, :].reshape(LATENT, LANES)
     values = jnp.zeros((ROWS, LANES), f32)
     for i in range(LTILES):
         numerator = jnp.sum(factor * rows[:, ROWS * i : ROWS * (i + 1), :], axis=0)
@@ -250,13 +285,16 @@
 
     first = pl.pallas_call(
         attend_kernel,
-        out_shape=jax.ShapeDtypeStruct((MEMBERS, CACHE + CHUNK, LANES), bf16),
-        in_specs=[SMEM, VMEM, VMEM, ANY, ANY, VMEM],
-        out_specs=VMEM,
+        out_shape=jax.ShapeDtypeStruct((MEMBERS, SENT, LANES), bf16),
+        in_specs=[SMEM, VMEM, ANY, ANY, ANY, ANY],
+        out_specs=ANY,
         scratch_shapes=[
+            pltpu.VMEM((REQ, STEPS * HEADS, WIDTH), bf16),
             pltpu.VMEM((REQ, WIDTH, SLICE), bf16),
             pltpu.VMEM((REQ, WIDTH, SLICE), bf16),
-            pltpu.SemaphoreType.DMA((2, REQ)),
+            pltpu.VMEM((MEMBERS, VROWS, LANES), bf16),
+            pltpu.VMEM((MEMBERS, SENT, LANES), bf16),
+            pltpu.SemaphoreType.DMA((3, REQ)),
         ],
         name="attend",
     )(lengths, new_entries, q, staying, leaving, w_value)
@@ -267,6 +305,7 @@
         out_shape=jax.ShapeDtypeStruct((MEMBERS, CHUNK + ROWS, LANES), bf16),
         in_specs=[SMEM, VMEM],
         out_specs=VMEM,
+        compiler_params=grant(4),
         name="merge",
     )(pairing, arrived)
     handed = lax.all_to_all(second, "context", 0, 0)
@@ -280,6 +319,7 @@
         ),
         in_specs=[VMEM, VMEM],
         out_specs=(VMEM, VMEM, VMEM),
+        compiler_params=grant(4),
         name="project",
     )(handed, w_out.T)
 
@@ -298,6 +338,7 @@
         out_specs=ANY,
         scratch_shapes=[pltpu.SemaphoreType.DMA, pltpu.SemaphoreType.DMA((2, PIECES))],
         cost_estimate=pl.CostEstimate(flops=0, bytes_accessed=8_000_000, transcendentals=0),
+        compiler_params=grant(1),
         name="keep",
     )(staying, forth)
     cache, near_total = pl.pallas_call(
@@ -308,6 +349,7 @@
         scratch_shapes=[pltpu.SemaphoreType.DMA((4, PIECES))],
         input_output_aliases={0: 0},
         cost_estimate=pl.CostEstimate(flops=0, bytes_accessed=4_000_000, transcendentals=0),
+        compiler_params=grant(1),
         name="near",
     )(cache, from_left, from_right, mine)
     cache, attn_out = pl.pallas_call(
@@ -317,6 +359,7 @@
         out_specs=(ANY, VMEM),
         scratch_shapes=[pltpu.SemaphoreType.DMA((2, PIECES))],
         input_output_aliases={0: 0},
+        compiler_params=grant(1),
         name="far",
     )(cache, far_left, far_right, near_total)
     attn_out = attn_out.reshape(REQ, STEPS, OUTC)

time: 92.7 us -> 87.8 us (0.947)
  the two profiles are of different devices: /device:TPU:146 before, /device:TPU:80 now
where the time goes in v4:
time: 87.8 us; the launch traced here: 87.4 us
  blocking collectives  44.3 us (50%)
  waiting for transfers between devices  17 us (19%)
  starting transfers between devices  15.4 us (18%)
  Pallas kernels  10 us (11%)
    all_to_all x1, blocking collectives, body(): arrived = lax.all_to_all(first, 'context', 0, 0)  28.5 us
    all_to_all x1, blocking collectives, body(): handed = lax.all_to_all(second, 'context', 0, 0)  15.8 us
    ppermute x1, waiting for transfers between devices, body(): from_left = lax.ppermute(forth, 'tensor', up)  9.71 us
    ppermute x1, waiting for transfers between devices, body(): far_right = lax.ppermute(from_right[BACK_1:], 'tensor', down)  7.25 us
    ppermute x1, starting transfers between devices, body(): far_left = lax.ppermute(from_left[0:FORTH_FAR + PART], 'tensor', up)  6.69 us
    pallas_call x1, Pallas kernels, body(): pl.pallas_call(attend_kernel, out_shape=jax.ShapeDtypeStruct((MEMBERS, SE...  5.09 us
    ppermute x1, starting transfers between devices, body(): from_left = lax.ppermute(forth, 'tensor', up)  4.83 us
    ppermute x1, starting transfers between devices, body(): from_right = lax.ppermute(back, 'tensor', down)  1.92 us
  transfers between devices with their start and end apart: 4, of which 2 were waited for; matrix products, arithmetic and copies ran while one was open for 0% of the time, Pallas kernels for 2%

profile of v4, /device:TPU:80, one launch (start us, length us, event | category | flops | bytes accessed | tf_op | source)
XLA Modules:
  0.0 87.4 jit_solution(8066094936726333916)
XLA Ops:
  0.6 0.0 copy-start.2
  0.6 0.0 copy-start.1
  0.7 5.1 %attend.1 = bf16[16,144,128]{2,1,0:T(8,128)(2,1)} custom-call(s32[4]{0:T(128)} %lengths.1, bf16[4,2,576]{2,1,0:T(2,128)(2,1)} %entries.1, bf16[4,32,576]{2,1,0:T(8,128)(2,1)} %bitcast.17, bf16[4,576,256]{2,1,0:T(8,128)(2,1)} %bitcast.12, bf16[4,576,256]{2,1,0:T(8,128)(2,1)} %bitcast.16, bf16[16,32,128]{2,1,0:T(8,128)(2,1)} %w_value_hbm.1), custom_call_target="tpu_custom_call" | custom-call | tf_op jit(solution)/shard_map/attend/pallas_call | solution.py:286
  5.7 28.5 %all_to_all.10.arrived = bf16[16,144,128]{2,1,0:T(8,128)(2,1)S(1)} all-to-all(bf16[16,144,128]{2,1,0:T(8,128)(2,1)} %attend.1), channel_id=1, replica_groups=mesh['dp'=8,'context'=16,'tensor'=4] {'context'}, dimensions={0} | all-to-all | bytes 1179648 | tf_op jit(solution)/shard_map/all_to_all | solution.py:301
  34.2 0.0 copy-done.2
  34.2 0.0 copy-start
  34.2 0.9 %merge.1 = bf16[16,80,128]{2,1,0:T(8,128)(2,1)S(1)} custom-call(s32[4,16]{1,0:T(4,128)S(1)} %copy-done.2, bf16[16,144,128]{2,1,0:T(8,128)(2,1)S(1)} %all_to_all.10.arrived), custom_call_target="tpu_custom_call" | custom-call | tf_op jit(solution)/shard_map/merge/pallas_call | solution.py:303
  35.2 15.8 %all_to_all.11.handed = bf16[16,80,128]{2,1,0:T(8,128)(2,1)S(1)} all-to-all(bf16[16,80,128]{2,1,0:T(8,128)(2,1)S(1)} %merge.1), channel_id=1, replica_groups=mesh['dp'=8,'context'=16,'tensor'=4] {'context'}, dimensions={0} | all-to-all | bytes 655360 | tf_op jit(solution)/shard_map/all_to_all | solution.py:311
  51.0 0.0 copy-done.1
  51.0 0.7 project.1
  51.7 4.8 %collective-permute-start = (bf16[1184,128]{1,0:T(8,128)(2,1)S(1)}, bf16[1184,128]{1,0:T(8,128)(2,1)S(1)}, u32[]{:S(2)}, u32[]{:S(2)}) collective-permute-start(bf16[1184,128]{1,0:T(8,128)(2,1)S(1)} %get-tuple-element.9.forth), channel_id=1, source_target_pairs={{3,0},{0,1},{1,2},{2,3},{7,4},{4,5},{5,6},{6,7},{11,8},{8,9},{9,10... | collective-permute-start | bytes 909320 | tf_op jit(solution)/shard_map/ppermute | solution.py:328
  56.5 1.9 %collective-permute-start.1 = (bf16[1168,128]{1,0:T(8,128)(2,1)S(1)}, bf16[1168,128]{1,0:T(8,128)(2,1)S(1)}, u32[]{:S(2)}, u32[]{:S(2)}) collective-permute-start(bf16[1168,128]{1,0:T(8,128)(2,1)S(1)} %get-tuple-element.10), channel_id=1, source_target_pairs={{1,0},{2,1},{3,2},{0,3},{5,4},{6,5},{7,6},{4,7},{9,8},{10,9},{11,1... | collective-permute-start | bytes 897032 | tf_op jit(solution)/shard_map/ppermute | solution.py:329
  58.4 9.7 %collective-permute-done.from_left = bf16[1184,128]{1,0:T(8,128)(2,1)S(1)} collective-permute-done((bf16[1184,128]{1,0:T(8,128)(2,1)S(1)}, bf16[1184,128]{1,0:T(8,128)(2,1)S(1)}, u32[]{:S(2)}, u32[]{:S(2)}) %collective-permute-start) | collective-permute-done | bytes 303136 | tf_op jit(solution)/shard_map/ppermute | solution.py:328
  68.2 6.7 %collective-permute-start.2 = (bf16[592,128]{1,0:T(8,128)(2,1)S(1)}, bf16[592,128]{1,0:T(8,128)(2,1)S(1)}, u32[]{:S(2)}, u32[]{:S(2)}) collective-permute-start(bf16[592,128]{1,0:T(8,128)(2,1)S(1)} %slice.8), channel_id=1, source_target_pairs={{3,0},{0,1},{1,2},{2,3},{7,4},{4,5},{5,6},{6,7},{11,8},{8,9},{9,10... | collective-permute-start | bytes 454664 | tf_op jit(solution)/shard_map/ppermute | solution.py:330
  74.9 0.0 collective-permute-done.1.from_right
  74.9 1.9 %collective-permute-start.3 = (bf16[576,128]{1,0:T(8,128)(2,1)S(1)}, bf16[576,128]{1,0:T(8,128)(2,1)S(1)}, u32[]{:S(2)}, u32[]{:S(2)}) collective-permute-start(bf16[576,128]{1,0:T(8,128)(2,1)S(1)} %slice.9), channel_id=1, source_target_pairs={{1,0},{2,1},{3,2},{0,3},{5,4},{6,5},{7,6},{4,7},{9,8},{10,9},{11,1... | collective-permute-start | bytes 442376 | tf_op jit(solution)/shard_map/ppermute | solution.py:331
  76.8 0.0 copy-done
  76.8 1.1 %keep.1.cache_in = bf16[4,576,512]{2,1,0:T(8,128)(2,1)} custom-call(bf16[4,576,256]{2,1,0:T(8,128)(2,1)S(1)} %bitcast.13, bf16[1184,128]{1,0:T(8,128)(2,1)S(1)} %get-tuple-element.9.forth), custom_call_target="tpu_custom_call" | custom-call | bytes 8000000 | tf_op jit(solution)/shard_map/keep/pallas_call | solution.py:334
  78.0 0.9 %near.1 = (bf16[4,576,512]{2,1,0:T(8,128)(2,1)}, f32[8,128]{1,0:T(8,128)S(1)}) custom-call(bf16[4,576,512]{2,1,0:T(8,128)(2,1)} %keep.1.cache_in, bf16[1184,128]{1,0:T(8,128)(2,1)S(1)} %collective-permute-done.from_left, bf16[1168,128]{1,0:T(8,128)(2,1)S(1)} %collective-permute-done.1.from_right, ...), custom_call_target="tpu_custom_call", output_to_operand_aliasing={{0}: (0, {})} | custom-call | bytes 4000000 | tf_op jit(solution)/shard_map/near/pallas_call | solution.py:344
  78.9 7.2 %collective-permute-done.3.far_right = bf16[576,128]{1,0:T(8,128)(2,1)S(1)} collective-permute-done((bf16[576,128]{1,0:T(8,128)(2,1)S(1)}, bf16[576,128]{1,0:T(8,128)(2,1)S(1)}, u32[]{:S(2)}, u32[]{:S(2)}) %collective-permute-start.3) | collective-permute-done | bytes 147488 | tf_op jit(solution)/shard_map/ppermute | solution.py:331
  86.1 0.0 collective-permute-done.2.far_left
  86.1 1.3 %far.1 = (bf16[4,576,512]{2,1,0:T(8,128)(2,1)}, bf16[8,112]{1,0:T(8,128)(2,1)}) custom-call(bf16[4,576,512]{2,1,0:T(8,128)(2,1)} %get-tuple-element.12.cache_in, bf16[592,128]{1,0:T(8,128)(2,1)S(1)} %collective-permute-done.2.far_left, bf16[576,128]{1,0:T(8,128)(2,1)S(1)} %collective-permute-done.3.far_right, ...), custom_call_target="tpu_custom_call", output_to_operand_aliasing={{0}: (0, {})} | custom-call | tf_op jit(solution)/shard_map/far/pallas_call | solution.py:355
  (2 shorter events, 0.0 us)
Async XLA Ops:
  0.6 33.6 %copy-start.2 = (s32[4,16]{1,0:T(4,128)S(1)}, s32[4,16]{1,0:T(4,128)}, u32[]{:S(2)}) copy-start(s32[4,16]{1,0:T(4,128)} %pairing.1) | copy-start | bytes 772
  0.6 50.3 %copy-start.1 = (bf16[2048,448]{0,1:T(8,128)(2,1)S(1)}, bf16[2048,448]{0,1:T(8,128)(2,1)}, u32[]{:S(2)}) copy-start(bf16[2048,448]{0,1:T(8,128)(2,1)} %param.15) | copy-start | bytes 5505028
  34.2 42.6 %copy-start = (bf16[1,4,256,576]{2,3,1,0:T(8,128)(2,1)S(1)}, bf16[1,4,256,576]{2,3,1,0:T(8,128)(2,1)}, u32[]{:S(2)}) copy-start(bf16[1,4,256,576]{2,3,1,0:T(8,128)(2,1)} %param.8) | copy-start | bytes 3538948
  51.7 16.5 %collective-permute-start = (bf16[1184,128]{1,0:T(8,128)(2,1)S(1)}, bf16[1184,128]{1,0:T(8,128)(2,1)S(1)}, u32[]{:S(2)}, u32[]{:S(2)}) collective-permute-start(bf16[1184,128]{1,0:T(8,128)(2,1)S(1)} %get-tuple-element.9.forth), channel_id=1, source_target_pairs={{3,0},{0,1},{1,2},{2,3},{7,4},{4,5},{5,6},{6,7},{11,8},{8,9},{9,10... | collective-permute-start | bytes 909320 | tf_op jit(solution)/shard_map/ppermute | solution.py:328
  56.5 18.4 %collective-permute-start.1 = (bf16[1168,128]{1,0:T(8,128)(2,1)S(1)}, bf16[1168,128]{1,0:T(8,128)(2,1)S(1)}, u32[]{:S(2)}, u32[]{:S(2)}) collective-permute-start(bf16[1168,128]{1,0:T(8,128)(2,1)S(1)} %get-tuple-element.10), channel_id=1, source_target_pairs={{1,0},{2,1},{3,2},{0,3},{5,4},{6,5},{7,6},{4,7},{9,8},{10,9},{11,1... | collective-permute-start | bytes 897032 | tf_op jit(solution)/shard_map/ppermute | solution.py:329
  68.2 18.0 %collective-permute-start.2 = (bf16[592,128]{1,0:T(8,128)(2,1)S(1)}, bf16[592,128]{1,0:T(8,128)(2,1)S(1)}, u32[]{:S(2)}, u32[]{:S(2)}) collective-permute-start(bf16[592,128]{1,0:T(8,128)(2,1)S(1)} %slice.8), channel_id=1, source_target_pairs={{3,0},{0,1},{1,2},{2,3},{7,4},{4,5},{5,6},{6,7},{11,8},{8,9},{9,10... | collective-permute-start | bytes 454664 | tf_op jit(solution)/shard_map/ppermute | solution.py:330
  74.9 11.2 %collective-permute-start.3 = (bf16[576,128]{1,0:T(8,128)(2,1)S(1)}, bf16[576,128]{1,0:T(8,128)(2,1)S(1)}, u32[]{:S(2)}, u32[]{:S(2)}) collective-permute-start(bf16[576,128]{1,0:T(8,128)(2,1)S(1)} %slice.9), channel_id=1, source_target_pairs={{1,0},{2,1},{3,2},{0,3},{5,4},{6,5},{7,6},{4,7},{9,8},{10,9},{11,1... | collective-permute-start | bytes 442376 | tf_op jit(solution)/shard_map/ppermute | solution.py:331

commit v5 on v4

--- a/solution.py
+++ b/solution.py
@@ -56,13 +56,15 @@
 
 
 def attend_kernel(
-    lengths,
-    entries,
+    lengths_hbm,
+    entries_hbm,
     queries_hbm,
     staying_hbm,
     leaving_hbm,
     w_value_hbm,
     out_hbm,
+    lengths,
+    entries,
     queries,
     staying,
     leaving,
@@ -78,6 +80,10 @@
             pltpu.make_async_copy(leaving_hbm.at[b], leaving.at[b], sems.at[0, b])
         )
         moved_copies[b].start()
+    length_copy = pltpu.make_async_copy(lengths_hbm, lengths, sems.at[3, 0])
+    length_copy.start()
+    entry_copy = pltpu.make_async_copy(entries_hbm, entries, sems.at[3, 1])
+    entry_copy.start()
     query_copy = pltpu.make_async_copy(queries_hbm, queries, sems.at[2, 0])
     query_copy.start()
     value_copy = pltpu.make_async_copy(w_value_hbm, w_value, sems.at[2, 1])
@@ -94,6 +100,8 @@
     step = (row >= HEADS).astype(jnp.int32)
     lane = lax.broadcasted_iota(jnp.int32, (STEPS * HEADS, LANES), 1)
     parts = []
+    length_copy.wait()
+    entry_copy.wait()
     for b in range(REQ):
         moved_copies[b].wait()
         new_slot = lengths[b] - first_moved
@@ -286,15 +294,17 @@
     first = pl.pallas_call(
         attend_kernel,
         out_shape=jax.ShapeDtypeStruct((MEMBERS, SENT, LANES), bf16),
-        in_specs=[SMEM, VMEM, ANY, ANY, ANY, ANY],
+        in_specs=[ANY] * 6,
         out_specs=ANY,
         scratch_shapes=[
+            pltpu.SMEM((REQ,), jnp.int32),
+            pltpu.VMEM((REQ, STEPS, WIDTH), bf16),
             pltpu.VMEM((REQ, STEPS * HEADS, WIDTH), bf16),
             pltpu.VMEM((REQ, WIDTH, SLICE), bf16),
             pltpu.VMEM((REQ, WIDTH, SLICE), bf16),
             pltpu.VMEM((MEMBERS, VROWS, LANES), bf16),
             pltpu.VMEM((MEMBERS, SENT, LANES), bf16),
-            pltpu.SemaphoreType.DMA((3, REQ)),
+            pltpu.SemaphoreType.DMA((4, REQ)),
         ],
         name="attend",
     )(lengths, new_entries, q, staying, leaving, w_value)

time: 87.8 us -> 86.9 us (0.990)
  the two profiles are of different devices: /device:TPU:80 before, /device:TPU:82 now
where the time goes in v5:
time: 86.9 us; the launch traced here: 86.5 us
  blocking collectives  44.1 us (51%)
  waiting for transfers between devices  17 us (20%)
  starting transfers between devices  15.4 us (18%)
  Pallas kernels  9.37 us (11%)
    all_to_all x1, blocking collectives, body(): arrived = lax.all_to_all(first, 'context', 0, 0)  28.3 us
    all_to_all x1, blocking collectives, body(): handed = lax.all_to_all(second, 'context', 0, 0)  15.8 us
    ppermute x1, waiting for transfers between devices, body(): from_left = lax.ppermute(forth, 'tensor', up)  9.69 us
    ppermute x1, waiting for transfers between devices, body(): far_right = lax.ppermute(from_right[BACK_1:], 'tensor', down)  7.26 us
    ppermute x1, starting transfers between devices, body(): far_left = lax.ppermute(from_left[0:FORTH_FAR + PART], 'tensor', up)  6.69 us
    ppermute x1, starting transfers between devices, body(): from_left = lax.ppermute(forth, 'tensor', up)  4.81 us
    pallas_call x1, Pallas kernels, body(): pl.pallas_call(attend_kernel, out_shape=jax.ShapeDtypeStruct((MEMBERS, SE...  4.42 us
    ppermute x1, starting transfers between devices, body(): from_right = lax.ppermute(back, 'tensor', down)  1.93 us
  transfers between devices with their start and end apart: 4, of which 2 were waited for; matrix products, arithmetic and copies ran while one was open for 0% of the time, Pallas kernels for 2%

profile of v5, /device:TPU:82, one launch (start us, length us, event | category | flops | bytes accessed | tf_op | source)
XLA Modules:
  0.0 86.5 jit_solution(9558697392764279396)
XLA Ops:
  0.6 0.0 copy-start.2
  0.6 0.0 copy-start.1
  0.7 4.4 %attend.1 = bf16[16,144,128]{2,1,0:T(8,128)(2,1)} custom-call(s32[4]{0:T(128)} %lengths_hbm.1, bf16[4,2,576]{2,1,0:T(2,128)(2,1)} %entries_hbm.1, bf16[4,32,576]{2,1,0:T(8,128)(2,1)} %bitcast.17, bf16[4,576,256]{2,1,0:T(8,128)(2,1)} %bitcast.12, bf16[4,576,256]{2,1,0:T(8,128)(2,1)} %bitcast.16, bf16[16,32,128]{2,1,0:T(8,128)(2,1)} %w_value_hbm.1), custom_call_target="tpu_custom_call" | custom-call | tf_op jit(solution)/shard_map/attend/pallas_call | solution.py:294
  5.1 28.3 %all_to_all.10.arrived = bf16[16,144,128]{2,1,0:T(8,128)(2,1)S(1)} all-to-all(bf16[16,144,128]{2,1,0:T(8,128)(2,1)} %attend.1), channel_id=1, replica_groups=mesh['dp'=8,'context'=16,'tensor'=4] {'context'}, dimensions={0} | all-to-all | bytes 1179648 | tf_op jit(solution)/shard_map/all_to_all | solution.py:311
  33.4 0.0 copy-done.2
  33.4 0.0 copy-start
  33.4 0.9 %merge.1 = bf16[16,80,128]{2,1,0:T(8,128)(2,1)S(1)} custom-call(s32[4,16]{1,0:T(4,128)S(1)} %copy-done.2, bf16[16,144,128]{2,1,0:T(8,128)(2,1)S(1)} %all_to_all.10.arrived), custom_call_target="tpu_custom_call" | custom-call | tf_op jit(solution)/shard_map/merge/pallas_call | solution.py:313
  34.3 15.8 %all_to_all.11.handed = bf16[16,80,128]{2,1,0:T(8,128)(2,1)S(1)} all-to-all(bf16[16,80,128]{2,1,0:T(8,128)(2,1)S(1)} %merge.1), channel_id=1, replica_groups=mesh['dp'=8,'context'=16,'tensor'=4] {'context'}, dimensions={0} | all-to-all | bytes 655360 | tf_op jit(solution)/shard_map/all_to_all | solution.py:321
  50.1 0.0 copy-done.1
  50.1 0.7 project.1
  50.8 4.8 %collective-permute-start = (bf16[1184,128]{1,0:T(8,128)(2,1)S(1)}, bf16[1184,128]{1,0:T(8,128)(2,1)S(1)}, u32[]{:S(2)}, u32[]{:S(2)}) collective-permute-start(bf16[1184,128]{1,0:T(8,128)(2,1)S(1)} %get-tuple-element.9.forth), channel_id=1, source_target_pairs={{3,0},{0,1},{1,2},{2,3},{7,4},{4,5},{5,6},{6,7},{11,8},{8,9},{9,10... | collective-permute-start | bytes 909320 | tf_op jit(solution)/shard_map/ppermute | solution.py:338
  55.6 1.9 %collective-permute-start.1 = (bf16[1168,128]{1,0:T(8,128)(2,1)S(1)}, bf16[1168,128]{1,0:T(8,128)(2,1)S(1)}, u32[]{:S(2)}, u32[]{:S(2)}) collective-permute-start(bf16[1168,128]{1,0:T(8,128)(2,1)S(1)} %get-tuple-element.10), channel_id=1, source_target_pairs={{1,0},{2,1},{3,2},{0,3},{5,4},{6,5},{7,6},{4,7},{9,8},{10,9},{11,1... | collective-permute-start | bytes 897032 | tf_op jit(solution)/shard_map/ppermute | solution.py:339
  57.5 9.7 %collective-permute-done.from_left = bf16[1184,128]{1,0:T(8,128)(2,1)S(1)} collective-permute-done((bf16[1184,128]{1,0:T(8,128)(2,1)S(1)}, bf16[1184,128]{1,0:T(8,128)(2,1)S(1)}, u32[]{:S(2)}, u32[]{:S(2)}) %collective-permute-start) | collective-permute-done | bytes 303136 | tf_op jit(solution)/shard_map/ppermute | solution.py:338
  67.2 6.7 %collective-permute-start.2 = (bf16[592,128]{1,0:T(8,128)(2,1)S(1)}, bf16[592,128]{1,0:T(8,128)(2,1)S(1)}, u32[]{:S(2)}, u32[]{:S(2)}) collective-permute-start(bf16[592,128]{1,0:T(8,128)(2,1)S(1)} %slice.8), channel_id=1, source_target_pairs={{3,0},{0,1},{1,2},{2,3},{7,4},{4,5},{5,6},{6,7},{11,8},{8,9},{9,10... | collective-permute-start | bytes 454664 | tf_op jit(solution)/shard_map/ppermute | solution.py:340
  73.9 0.0 collective-permute-done.1.from_right
  74.0 1.9 %collective-permute-start.3 = (bf16[576,128]{1,0:T(8,128)(2,1)S(1)}, bf16[576,128]{1,0:T(8,128)(2,1)S(1)}, u32[]{:S(2)}, u32[]{:S(2)}) collective-permute-start(bf16[576,128]{1,0:T(8,128)(2,1)S(1)} %slice.9), channel_id=1, source_target_pairs={{1,0},{2,1},{3,2},{0,3},{5,4},{6,5},{7,6},{4,7},{9,8},{10,9},{11,1... | collective-permute-start | bytes 442376 | tf_op jit(solution)/shard_map/ppermute | solution.py:341
  75.9 0.0 copy-done
  75.9 1.1 %keep.1.cache_in = bf16[4,576,512]{2,1,0:T(8,128)(2,1)} custom-call(bf16[4,576,256]{2,1,0:T(8,128)(2,1)S(1)} %bitcast.13, bf16[1184,128]{1,0:T(8,128)(2,1)S(1)} %get-tuple-element.9.forth), custom_call_target="tpu_custom_call" | custom-call | bytes 8000000 | tf_op jit(solution)/shard_map/keep/pallas_call | solution.py:344
  77.1 0.9 %near.1 = (bf16[4,576,512]{2,1,0:T(8,128)(2,1)}, f32[8,128]{1,0:T(8,128)S(1)}) custom-call(bf16[4,576,512]{2,1,0:T(8,128)(2,1)} %keep.1.cache_in, bf16[1184,128]{1,0:T(8,128)(2,1)S(1)} %collective-permute-done.from_left, bf16[1168,128]{1,0:T(8,128)(2,1)S(1)} %collective-permute-done.1.from_right, ...), custom_call_target="tpu_custom_call", output_to_operand_aliasing={{0}: (0, {})} | custom-call | bytes 4000000 | tf_op jit(solution)/shard_map/near/pallas_call | solution.py:354
  77.9 7.3 %collective-permute-done.3.far_right = bf16[576,128]{1,0:T(8,128)(2,1)S(1)} collective-permute-done((bf16[576,128]{1,0:T(8,128)(2,1)S(1)}, bf16[576,128]{1,0:T(8,128)(2,1)S(1)}, u32[]{:S(2)}, u32[]{:S(2)}) %collective-permute-start.3) | collective-permute-done | bytes 147488 | tf_op jit(solution)/shard_map/ppermute | solution.py:341
  85.2 0.0 collective-permute-done.2.far_left
  85.2 1.3 %far.1 = (bf16[4,576,512]{2,1,0:T(8,128)(2,1)}, bf16[8,112]{1,0:T(8,128)(2,1)}) custom-call(bf16[4,576,512]{2,1,0:T(8,128)(2,1)} %get-tuple-element.12.cache_in, bf16[592,128]{1,0:T(8,128)(2,1)S(1)} %collective-permute-done.2.far_left, bf16[576,128]{1,0:T(8,128)(2,1)S(1)} %collective-permute-done.3.far_right, ...), custom_call_target="tpu_custom_call", output_to_operand_aliasing={{0}: (0, {})} | custom-call | tf_op jit(solution)/shard_map/far/pallas_call | solution.py:365
  (2 shorter events, 0.0 us)
Async XLA Ops:
  0.6 32.8 %copy-start.2 = (s32[4,16]{1,0:T(4,128)S(1)}, s32[4,16]{1,0:T(4,128)}, u32[]{:S(2)}) copy-start(s32[4,16]{1,0:T(4,128)} %pairing.1) | copy-start | bytes 772
  0.6 49.5 %copy-start.1 = (bf16[2048,448]{0,1:T(8,128)(2,1)S(1)}, bf16[2048,448]{0,1:T(8,128)(2,1)}, u32[]{:S(2)}) copy-start(bf16[2048,448]{0,1:T(8,128)(2,1)} %param.15) | copy-start | bytes 5505028
  33.4 42.5 %copy-start = (bf16[1,4,256,576]{2,3,1,0:T(8,128)(2,1)S(1)}, bf16[1,4,256,576]{2,3,1,0:T(8,128)(2,1)}, u32[]{:S(2)}) copy-start(bf16[1,4,256,576]{2,3,1,0:T(8,128)(2,1)} %param.8) | copy-start | bytes 3538948
  50.8 16.4 %collective-permute-start = (bf16[1184,128]{1,0:T(8,128)(2,1)S(1)}, bf16[1184,128]{1,0:T(8,128)(2,1)S(1)}, u32[]{:S(2)}, u32[]{:S(2)}) collective-permute-start(bf16[1184,128]{1,0:T(8,128)(2,1)S(1)} %get-tuple-element.9.forth), channel_id=1, source_target_pairs={{3,0},{0,1},{1,2},{2,3},{7,4},{4,5},{5,6},{6,7},{11,8},{8,9},{9,10... | collective-permute-start | bytes 909320 | tf_op jit(solution)/shard_map/ppermute | solution.py:338
  55.6 18.3 %collective-permute-start.1 = (bf16[1168,128]{1,0:T(8,128)(2,1)S(1)}, bf16[1168,128]{1,0:T(8,128)(2,1)S(1)}, u32[]{:S(2)}, u32[]{:S(2)}) collective-permute-start(bf16[1168,128]{1,0:T(8,128)(2,1)S(1)} %get-tuple-element.10), channel_id=1, source_target_pairs={{1,0},{2,1},{3,2},{0,3},{5,4},{6,5},{7,6},{4,7},{9,8},{10,9},{11,1... | collective-permute-start | bytes 897032 | tf_op jit(solution)/shard_map/ppermute | solution.py:339
  67.2 18.0 %collective-permute-start.2 = (bf16[592,128]{1,0:T(8,128)(2,1)S(1)}, bf16[592,128]{1,0:T(8,128)(2,1)S(1)}, u32[]{:S(2)}, u32[]{:S(2)}) collective-permute-start(bf16[592,128]{1,0:T(8,128)(2,1)S(1)} %slice.8), channel_id=1, source_target_pairs={{3,0},{0,1},{1,2},{2,3},{7,4},{4,5},{5,6},{6,7},{11,8},{8,9},{9,10... | collective-permute-start | bytes 454664 | tf_op jit(solution)/shard_map/ppermute | solution.py:340
  74.0 11.2 %collective-permute-start.3 = (bf16[576,128]{1,0:T(8,128)(2,1)S(1)}, bf16[576,128]{1,0:T(8,128)(2,1)S(1)}, u32[]{:S(2)}, u32[]{:S(2)}) collective-permute-start(bf16[576,128]{1,0:T(8,128)(2,1)S(1)} %slice.9), channel_id=1, source_target_pairs={{1,0},{2,1},{3,2},{0,3},{5,4},{6,5},{7,6},{4,7},{9,8},{10,9},{11,1... | collective-permute-start | bytes 442376 | tf_op jit(solution)/shard_map/ppermute | solution.py:341

commit v6 on v5

--- a/solution.py
+++ b/solution.py
@@ -27,11 +27,11 @@
 PART = 2 * ROWS
 PIECES = 2
 PIECE = WIDTH // PIECES
-FORTH_0 = 0
-FORTH_FAR = WIDTH
-FORTH_NEAR = FORTH_FAR + PART
-FORTH_1 = FORTH_NEAR + PART
-FORTH_ROWS = FORTH_1 + WIDTH
+FORTH_FAR = 0
+FORTH_0 = FORTH_FAR + PART
+FORTH_1 = FORTH_0 + WIDTH
+FORTH_NEAR = FORTH_1 + WIDTH
+FORTH_ROWS = FORTH_NEAR + PART
 BACK_0 = PART
 BACK_1 = BACK_0 + WIDTH
 BACK_ROWS = BACK_1 + WIDTH
@@ -224,7 +224,7 @@
     back[0:PART, :] = pieces(part_of(3))
 
 
-def stores(block, first, cache, request, half, sems):
+def stores(block, first, cache, request, half, sems, pieces=range(PIECES)):
     lanes = SLICE + half * LANES
     return [
         pltpu.make_async_copy(
@@ -232,7 +232,7 @@
             cache.at[request, PIECE * i : PIECE * (i + 1), lanes : lanes + LANES],
             sems.at[i],
         )
-        for i in range(PIECES)
+        for i in pieces
     ]
 
 
@@ -276,8 +276,9 @@
 
 def far_kernel(cache_in, far_left, far_right, near_total, cache, attn, sems):
     across = lax.rem(lax.axis_index("tensor") + 2, TENSOR)
-    copies = stores(far_left, 0, cache, across, 0, sems.at[0])
-    copies += stores(far_right, 0, cache, across, 1, sems.at[1])
+    copies = stores(far_left, FORTH_0, cache, across, 0, sems.at[0])
+    copies += stores(far_left, FORTH_1, cache, across, 1, sems.at[1], [0])
+    copies += stores(far_right, -PIECE, cache, across, 1, sems.at[1], [1])
     for copy in copies:
         copy.start()
     total = near_total[...] + joined(far_left[FORTH_FAR : FORTH_FAR + PART, :])
@@ -337,8 +338,8 @@
     down = [((t + 1) % TENSOR, t) for t in range(TENSOR)]
     from_left = lax.ppermute(forth, "tensor", up)
     from_right = lax.ppermute(back, "tensor", down)
-    far_left = lax.ppermute(from_left[0 : FORTH_FAR + PART], "tensor", up)
-    far_right = lax.ppermute(from_right[BACK_1:], "tensor", down)
+    far_left = lax.ppermute(from_left[0 : FORTH_1 + PIECE], "tensor", up)
+    far_right = lax.ppermute(from_right[BACK_1 + PIECE :], "tensor", down)
 
     whole = jax.ShapeDtypeStruct((REQ, WIDTH, 2 * SLICE), bf16)
     cache = pl.pallas_call(

time: 86.9 us -> 85.3 us (0.982)
  the two profiles are of different devices: /device:TPU:82 before, /device:TPU:24 now
where the time goes in v6:
time: 85.3 us; the launch traced here: 84.6 us
  blocking collectives  43.8 us (51%)
  starting transfers between devices  16.2 us (19%)
  waiting for transfers between devices  14.4 us (17%)
  Pallas kernels  9.37 us (11%)
    all_to_all x1, blocking collectives, body(): arrived = lax.all_to_all(first, 'context', 0, 0)  30.3 us
    all_to_all x1, blocking collectives, body(): handed = lax.all_to_all(second, 'context', 0, 0)  13.6 us
    ppermute x1, waiting for transfers between devices, body(): from_left = lax.ppermute(forth, 'tensor', up)  10 us
    ppermute x1, starting transfers between devices, body(): far_left = lax.ppermute(from_left[0:FORTH_1 + PIECE], 'tensor', up)  7.54 us
    ppermute x1, starting transfers between devices, body(): from_left = lax.ppermute(forth, 'tensor', up)  4.81 us
    pallas_call x1, Pallas kernels, body(): pl.pallas_call(attend_kernel, out_shape=jax.ShapeDtypeStruct((MEMBERS, SE...  4.42 us
    ppermute x1, waiting for transfers between devices, body(): far_right = lax.ppermute(from_right[BACK_1 + PIECE:], 'tensor', down)  4.37 us
    ppermute x1, starting transfers between devices, body(): from_right = lax.ppermute(back, 'tensor', down)  1.93 us
  transfers between devices with their start and end apart: 4, of which 2 were waited for; matrix products, arithmetic and copies ran while one was open for 0% of the time, Pallas kernels for 2%

profile of v6, /device:TPU:24, one launch (start us, length us, event | category | flops | bytes accessed | tf_op | source)
XLA Modules:
  0.0 84.6 jit_solution(10122989975969991202)
XLA Ops:
  0.6 0.0 copy-start.2
  0.6 0.0 copy-start.1
  0.7 4.4 %attend.1 = bf16[16,144,128]{2,1,0:T(8,128)(2,1)} custom-call(s32[4]{0:T(128)} %lengths_hbm.1, bf16[4,2,576]{2,1,0:T(2,128)(2,1)} %entries_hbm.1, bf16[4,32,576]{2,1,0:T(8,128)(2,1)} %bitcast.17, bf16[4,576,256]{2,1,0:T(8,128)(2,1)} %bitcast.12, bf16[4,576,256]{2,1,0:T(8,128)(2,1)} %bitcast.16, bf16[16,32,128]{2,1,0:T(8,128)(2,1)} %w_value_hbm.1), custom_call_target="tpu_custom_call" | custom-call | tf_op jit(solution)/shard_map/attend/pallas_call | solution.py:295
  5.1 30.3 %all_to_all.10.arrived = bf16[16,144,128]{2,1,0:T(8,128)(2,1)S(1)} all-to-all(bf16[16,144,128]{2,1,0:T(8,128)(2,1)} %attend.1), channel_id=1, replica_groups=mesh['dp'=8,'context'=16,'tensor'=4] {'context'}, dimensions={0} | all-to-all | bytes 1179648 | tf_op jit(solution)/shard_map/all_to_all | solution.py:312
  35.4 0.0 copy-done.2
  35.4 0.0 copy-start
  35.4 0.9 %merge.1 = bf16[16,80,128]{2,1,0:T(8,128)(2,1)S(1)} custom-call(s32[4,16]{1,0:T(4,128)S(1)} %copy-done.2, bf16[16,144,128]{2,1,0:T(8,128)(2,1)S(1)} %all_to_all.10.arrived), custom_call_target="tpu_custom_call" | custom-call | tf_op jit(solution)/shard_map/merge/pallas_call | solution.py:314
  36.3 13.6 %all_to_all.11.handed = bf16[16,80,128]{2,1,0:T(8,128)(2,1)S(1)} all-to-all(bf16[16,80,128]{2,1,0:T(8,128)(2,1)S(1)} %merge.1), channel_id=1, replica_groups=mesh['dp'=8,'context'=16,'tensor'=4] {'context'}, dimensions={0} | all-to-all | bytes 655360 | tf_op jit(solution)/shard_map/all_to_all | solution.py:322
  49.9 0.0 copy-done.1
  49.9 0.7 project.1
  50.5 4.8 %collective-permute-start = (bf16[1184,128]{1,0:T(8,128)(2,1)S(1)}, bf16[1184,128]{1,0:T(8,128)(2,1)S(1)}, u32[]{:S(2)}, u32[]{:S(2)}) collective-permute-start(bf16[1184,128]{1,0:T(8,128)(2,1)S(1)} %get-tuple-element.9.forth), channel_id=1, source_target_pairs={{3,0},{0,1},{1,2},{2,3},{7,4},{4,5},{5,6},{6,7},{11,8},{8,9},{9,10... | collective-permute-start | bytes 909320 | tf_op jit(solution)/shard_map/ppermute | solution.py:339
  55.4 1.9 %collective-permute-start.1 = (bf16[1168,128]{1,0:T(8,128)(2,1)S(1)}, bf16[1168,128]{1,0:T(8,128)(2,1)S(1)}, u32[]{:S(2)}, u32[]{:S(2)}) collective-permute-start(bf16[1168,128]{1,0:T(8,128)(2,1)S(1)} %get-tuple-element.10), channel_id=1, source_target_pairs={{1,0},{2,1},{3,2},{0,3},{5,4},{6,5},{7,6},{4,7},{9,8},{10,9},{11,1... | collective-permute-start | bytes 897032 | tf_op jit(solution)/shard_map/ppermute | solution.py:340
  57.3 10.0 %collective-permute-done.from_left = bf16[1184,128]{1,0:T(8,128)(2,1)S(1)} collective-permute-done((bf16[1184,128]{1,0:T(8,128)(2,1)S(1)}, bf16[1184,128]{1,0:T(8,128)(2,1)S(1)}, u32[]{:S(2)}, u32[]{:S(2)}) %collective-permute-start) | collective-permute-done | bytes 303136 | tf_op jit(solution)/shard_map/ppermute | solution.py:339
  67.3 7.5 %collective-permute-start.2 = (bf16[880,128]{1,0:T(8,128)(2,1)S(1)}, bf16[880,128]{1,0:T(8,128)(2,1)S(1)}, u32[]{:S(2)}, u32[]{:S(2)}) collective-permute-start(bf16[880,128]{1,0:T(8,128)(2,1)S(1)} %slice.8), channel_id=1, source_target_pairs={{3,0},{0,1},{1,2},{2,3},{7,4},{4,5},{5,6},{6,7},{11,8},{8,9},{9,10... | collective-permute-start | bytes 675848 | tf_op jit(solution)/shard_map/ppermute | solution.py:341
  74.9 0.0 collective-permute-done.1.from_right
  74.9 1.9 %collective-permute-start.3 = (bf16[288,128]{1,0:T(8,128)(2,1)S(1)}, bf16[288,128]{1,0:T(8,128)(2,1)S(1)}, u32[]{:S(2)}, u32[]{:S(2)}) collective-permute-start(bf16[288,128]{1,0:T(8,128)(2,1)S(1)} %slice.9), channel_id=1, source_target_pairs={{1,0},{2,1},{3,2},{0,3},{5,4},{6,5},{7,6},{4,7},{9,8},{10,9},{11,1... | collective-permute-start | bytes 221192 | tf_op jit(solution)/shard_map/ppermute | solution.py:342
  76.8 0.0 copy-done
  76.8 1.1 %keep.1.cache_in = bf16[4,576,512]{2,1,0:T(8,128)(2,1)} custom-call(bf16[4,576,256]{2,1,0:T(8,128)(2,1)S(1)} %bitcast.13, bf16[1184,128]{1,0:T(8,128)(2,1)S(1)} %get-tuple-element.9.forth), custom_call_target="tpu_custom_call" | custom-call | bytes 8000000 | tf_op jit(solution)/shard_map/keep/pallas_call | solution.py:345
  78.0 0.9 %near.1 = (bf16[4,576,512]{2,1,0:T(8,128)(2,1)}, f32[8,128]{1,0:T(8,128)S(1)}) custom-call(bf16[4,576,512]{2,1,0:T(8,128)(2,1)} %keep.1.cache_in, bf16[1184,128]{1,0:T(8,128)(2,1)S(1)} %collective-permute-done.from_left, bf16[1168,128]{1,0:T(8,128)(2,1)S(1)} %collective-permute-done.1.from_right, ...), custom_call_target="tpu_custom_call", output_to_operand_aliasing={{0}: (0, {})} | custom-call | bytes 4000000 | tf_op jit(solution)/shard_map/near/pallas_call | solution.py:355
  78.9 4.4 %collective-permute-done.3.far_right = bf16[288,128]{1,0:T(8,128)(2,1)S(1)} collective-permute-done((bf16[288,128]{1,0:T(8,128)(2,1)S(1)}, bf16[288,128]{1,0:T(8,128)(2,1)S(1)}, u32[]{:S(2)}, u32[]{:S(2)}) %collective-permute-start.3) | collective-permute-done | bytes 73760 | tf_op jit(solution)/shard_map/ppermute | solution.py:342
  83.3 0.0 collective-permute-done.2.far_left
  83.3 1.3 %far.1 = (bf16[4,576,512]{2,1,0:T(8,128)(2,1)}, bf16[8,112]{1,0:T(8,128)(2,1)}) custom-call(bf16[4,576,512]{2,1,0:T(8,128)(2,1)} %get-tuple-element.12.cache_in, bf16[880,128]{1,0:T(8,128)(2,1)S(1)} %collective-permute-done.2.far_left, bf16[288,128]{1,0:T(8,128)(2,1)S(1)} %collective-permute-done.3.far_right, ...), custom_call_target="tpu_custom_call", output_to_operand_aliasing={{0}: (0, {})} | custom-call | tf_op jit(solution)/shard_map/far/pallas_call | solution.py:366
  (2 shorter events, 0.0 us)
Async XLA Ops:
  0.6 34.7 %copy-start.2 = (s32[4,16]{1,0:T(4,128)S(1)}, s32[4,16]{1,0:T(4,128)}, u32[]{:S(2)}) copy-start(s32[4,16]{1,0:T(4,128)} %pairing.1) | copy-start | bytes 772
  0.6 49.2 %copy-start.1 = (bf16[2048,448]{0,1:T(8,128)(2,1)S(1)}, bf16[2048,448]{0,1:T(8,128)(2,1)}, u32[]{:S(2)}) copy-start(bf16[2048,448]{0,1:T(8,128)(2,1)} %param.15) | copy-start | bytes 5505028
  35.4 41.5 %copy-start = (bf16[1,4,256,576]{2,3,1,0:T(8,128)(2,1)S(1)}, bf16[1,4,256,576]{2,3,1,0:T(8,128)(2,1)}, u32[]{:S(2)}) copy-start(bf16[1,4,256,576]{2,3,1,0:T(8,128)(2,1)} %param.8) | copy-start | bytes 3538948
  50.5 16.8 %collective-permute-start = (bf16[1184,128]{1,0:T(8,128)(2,1)S(1)}, bf16[1184,128]{1,0:T(8,128)(2,1)S(1)}, u32[]{:S(2)}, u32[]{:S(2)}) collective-permute-start(bf16[1184,128]{1,0:T(8,128)(2,1)S(1)} %get-tuple-element.9.forth), channel_id=1, source_target_pairs={{3,0},{0,1},{1,2},{2,3},{7,4},{4,5},{5,6},{6,7},{11,8},{8,9},{9,10... | collective-permute-start | bytes 909320 | tf_op jit(solution)/shard_map/ppermute | solution.py:339
  55.4 19.5 %collective-permute-start.1 = (bf16[1168,128]{1,0:T(8,128)(2,1)S(1)}, bf16[1168,128]{1,0:T(8,128)(2,1)S(1)}, u32[]{:S(2)}, u32[]{:S(2)}) collective-permute-start(bf16[1168,128]{1,0:T(8,128)(2,1)S(1)} %get-tuple-element.10), channel_id=1, source_target_pairs={{1,0},{2,1},{3,2},{0,3},{5,4},{6,5},{7,6},{4,7},{9,8},{10,9},{11,1... | collective-permute-start | bytes 897032 | tf_op jit(solution)/shard_map/ppermute | solution.py:340
  67.3 15.9 %collective-permute-start.2 = (bf16[880,128]{1,0:T(8,128)(2,1)S(1)}, bf16[880,128]{1,0:T(8,128)(2,1)S(1)}, u32[]{:S(2)}, u32[]{:S(2)}) collective-permute-start(bf16[880,128]{1,0:T(8,128)(2,1)S(1)} %slice.8), channel_id=1, source_target_pairs={{3,0},{0,1},{1,2},{2,3},{7,4},{4,5},{5,6},{6,7},{11,8},{8,9},{9,10... | collective-permute-start | bytes 675848 | tf_op jit(solution)/shard_map/ppermute | solution.py:341
  74.9 8.4 %collective-permute-start.3 = (bf16[288,128]{1,0:T(8,128)(2,1)S(1)}, bf16[288,128]{1,0:T(8,128)(2,1)S(1)}, u32[]{:S(2)}, u32[]{:S(2)}) collective-permute-start(bf16[288,128]{1,0:T(8,128)(2,1)S(1)} %slice.9), channel_id=1, source_target_pairs={{1,0},{2,1},{3,2},{0,3},{5,4},{6,5},{7,6},{4,7},{9,8},{10,9},{11,1... | collective-permute-start | bytes 221192 | tf_op jit(solution)/shard_map/ppermute | solution.py:342
